TPU v7x, 32 devices: a whole 2x2x4 slice. The times are simulated.
32 devices in a mesh: gx: 8 (over y, x, core), gy: 4 (over z).
Axes of the slice: x: 2, y: 2, z: 4, core: 2. Of those that a mesh axis runs over, the one named last changes fastest.
Arguments:
- labels: float32 [32768, 512], P(('gx', 'gy')), may hold values from -6 to 6
- point_order: int32 [32, 1024], P(('gx', 'gy')), may hold values from 0 to 1023, each once within a row
- leaf_inverse: float32 [32768, 1024], P(('gx', 'gy')), as said below
- leaf_basis: float32 [32768, 256], P(('gx', 'gy')), may hold values from -0.1875 to 0.1875
- couple_one: float32 [8192, 1024], P(('gx', 'gy'))
- transfer_one: float32 [8192, 256], P(('gx', 'gy')), may hold values from -0.1875 to 0.1875
- couple_two: float32 [2048, 1024], P(('gx', 'gy'))
- transfer_two: float32 [2048, 256], P(('gx', 'gy')), may hold values from -0.1875 to 0.1875
- couple_top: float32 [1024, 256], P(('gx', 'gy'))
Outputs:
- solution: float32 [32768, 512], P(('gx', 'gy'))
Inputs may be any that keep to these rules, and one draw needn't show every extreme that they name: Each row of point_order is a permutation of 0 to 1023. leaf_inverse, couple_one, couple_two and the top matrix assembled from couple_top are dense with a dominant diagonal.
All inputs are finite; a program needn't handle non-finite values.
Results may differ from a plain program's by a relative error of at most 0.00011.
Values sent between devices are 32-bit elements; how exact they have to be, the bound alone decides.
A program may use at most 64 MiB of HBM per device.

v0:
```python
import jax
import jax.numpy as jnp
from jax import lax
from jax.sharding import PartitionSpec as P


def from_partner(block, axis, distance):
    count = lax.axis_size(axis)
    route = []
    for low in range(count):
        high = low | 1 << distance
        if high != low and high < count:
            route += [(low, high), (high, low)]
    return lax.ppermute(block, axis, route)


def matmul(left, right):
    return jnp.dot(left, right, precision=lax.Precision.HIGHEST)


def matmul_left(left, right):
    return lax.dot_general(left, right, (((0,), (0,)), ((), ())), precision=lax.Precision.HIGHEST)


def doubling(block, bit_list, mover, axis_dim):
    device_index = lax.axis_index(("gx", "gy"))
    for bit_index in bit_list:
        other = mover(block, bit_index)
        upper = device_index >> bit_index & 1 == 1
        block = jnp.where(
            upper,
            jnp.concatenate([other, block], axis_dim),
            jnp.concatenate([block, other], axis_dim),
        )
    return block


def climb_mover(value, bit_index):
    return from_partner(value, ("gx", "gy"), bit_index)


def descend_mover(value, bit_index):
    return from_partner(value, ("gx", "gy"), bit_index)


def subtree_sum(partial_value, bit_list):
    for bit_index in bit_list:
        partial_value = partial_value + from_partner(partial_value, ("gx", "gy"), bit_index)
    return partial_value


def apply_transfer(transfer_rows, incoming, bit_list):

    def basis_mover(value, bit_index):
        return from_partner(value, ("gx", "gy"), bit_index)

    return matmul(doubling(transfer_rows, bit_list, basis_mover, 0), incoming)


def top_share(partial_value, slice_rows):
    device_index = lax.axis_index(("gx", "gy"))
    total_bits = lax.axis_size(("gx", "gy")).bit_length() - 1
    group_bits = tuple(range(4, total_bits))
    for bit_index in group_bits:
        partial_value = partial_value + from_partner(partial_value, ("gx", "gy"), bit_index)
    return lax.dynamic_slice_in_dim(partial_value, (device_index >> 4) * slice_rows, slice_rows, 0)


def per_device(
    labels,
    point_order,
    leaf_inverse,
    leaf_basis,
    couple_one,
    transfer_one,
    couple_two,
    transfer_two,
    couple_top,
):
    rank_width = leaf_basis.shape[1]
    slice_rows = rank_width // 16
    order_row = point_order[0]
    rhs = labels[order_row]
    solved = matmul(leaf_inverse, rhs)
    proj = matmul_left(leaf_basis, solved)
    stack_one = doubling(proj, (0, 1), climb_mover, 0)
    solve_one = matmul(couple_one, stack_one)
    reduced_one = subtree_sum(matmul_left(transfer_one, solve_one), (0, 1))
    stack_two = doubling(reduced_one, (2, 3), climb_mover, 0)
    solve_two = matmul(couple_two, stack_two)
    reduced_two = subtree_sum(matmul_left(transfer_two, solve_two), (0, 1, 2, 3))
    top_partial = matmul(couple_top, reduced_two)
    own_rows = top_share(top_partial, slice_rows)
    block_two = doubling(own_rows, (0, 1, 2, 3), descend_mover, 0)
    fixed_two = solve_two - matmul(
        couple_two, apply_transfer(transfer_two, block_two, (0, 1, 2, 3))
    )
    block_one = doubling(fixed_two, (0, 1), descend_mover, 0)
    fixed_one = solve_one - matmul(couple_one, apply_transfer(transfer_one, block_one, (0, 1)))
    correction = matmul(leaf_inverse, matmul(leaf_basis, fixed_one))
    tree_order = solved - correction
    return jnp.zeros_like(tree_order).at[order_row].set(tree_order)


def solution(mesh):
    in_specs = (
        P(("gx", "gy"), None),
        P(("gx", "gy"), None),
        P(("gx", "gy"), None),
        P(("gx", "gy"), None),
        P(("gx", "gy"), None),
        P(("gx", "gy"), None),
        P(("gx", "gy"), None),
        P(("gx", "gy"), None),
        P(("gx", "gy"), None),
    )
    out_specs = P(("gx", "gy"), None)
    return jax.shard_map(
        per_device, mesh=mesh, in_specs=in_specs, out_specs=out_specs, check_vma=False
    )
```

profile of v0, /device:TPU:0, one launch (start us, length us, event | category | flops | bytes accessed | tf_op | source)
XLA Modules:
  0.0 317.4 jit_solution(10330530635195715882)
XLA Ops:
  1.6 4.9 %gather_fusion = f32[1024,512]{1,0:T(8,128)} fusion(f32[1024,512]{1,0:T(8,128)S(1)} %copy-done, s32[1024]{0:T(1024)S(1)} %broadcast_clamp_fusion), kind=kCustom, calls=%fused_computation | custom fusion | bytes 4198400 | tf_op jit(solution)/shard_map/gather | solution.py:83
  6.5 16.1 %fusion.48 = f32[512,1024]{1,0:T(8,128)S(1)} fusion(f32[1024,512]{1,0:T(8,128)} %gather_fusion, f32[1024,1024]{1,0:T(8,128)} %param.11), kind=kOutput, calls=%fused_computation.76 | convolution fusion | flops 6442450944 | bytes 8388608 | tf_op jit(solution)/shard_map/dot_general | solution.py:18
  26.8 3.0 collective-permute-start
  29.8 12.2 %collective-permute-done = f32[256,512]{1,0:T(8,128)} collective-permute-done((f32[256,512]{1,0:T(8,128)}, f32[256,512]{1,0:T(8,128)}, u32[]{:S(2)}, u32[]{:S(2)}) %collective-permute-start) | collective-permute-done | bytes 524320 | tf_op jit(solution)/shard_map/ppermute | solution.py:14
  47.5 45.3 %collective-permute-done.1 = f32[512,512]{1,0:T(8,128)} collective-permute-done((f32[512,512]{1,0:T(8,128)}, f32[512,512]{1,0:T(8,128)}, u32[]{:S(2)}, u32[]{:S(2)}) %collective-permute-start.1) | collective-permute-done | bytes 1048608 | tf_op jit(solution)/shard_map/ppermute | solution.py:14
  92.8 5.9 %fusion = f32[512,256]{1,0:T(8,128)S(1)} fusion(f32[256,1024]{1,0:T(8,128)} %param.13, f32[512,512]{1,0:T(8,128)} %maximum_select_fusion.4, f32[512,512]{1,0:T(8,128)} %collective-permute-done.1, pred[]{:T(512)S(6)} %eq.8), kind=kOutput, calls=%fused_computation.3 | convolution fusion | flops 1612185600 | bytes 3670017 | tf_op jit(solution)/shard_map/dot_general | solution.py:18
  100.0 12.4 %collective-permute-done.4 = f32[256,512]{1,0:T(8,128)S(1)} collective-permute-done((f32[256,512]{1,0:T(8,128)S(1)}, f32[256,512]{1,0:T(8,128)S(1)}, u32[]{:S(2)}, u32[]{:S(2)}) %collective-permute-start.4) | collective-permute-done | bytes 524320 | tf_op jit(solution)/shard_map/ppermute | solution.py:14
  112.5 3.2 collective-permute-start.5
  115.7 22.8 %collective-permute-done.5 = f32[256,512]{1,0:T(8,128)S(1)} collective-permute-done((f32[256,512]{1,0:T(8,128)S(1)}, f32[256,512]{1,0:T(8,128)S(1)}, u32[]{:S(2)}, u32[]{:S(2)}) %collective-permute-start.5) | collective-permute-done | bytes 524320 | tf_op jit(solution)/shard_map/ppermute | solution.py:14
  145.8 24.0 %collective-permute-done.7 = f32[512,512]{1,0:T(8,128)} collective-permute-done((f32[512,512]{1,0:T(8,128)}, f32[512,512]{1,0:T(8,128)}, u32[]{:S(2)}, u32[]{:S(2)}) %collective-permute-start.7) | collective-permute-done | bytes 1048608 | tf_op jit(solution)/shard_map/ppermute | solution.py:14
  169.8 3.8 %fusion.6 = f32[512,64]{0,1:T(8,128)S(1)} fusion(f32[64,1024]{1,0:T(8,128)} %param.15, f32[512,512]{1,0:T(8,128)} %maximum_select_fusion.7, f32[512,512]{1,0:T(8,128)} %collective-permute-done.7, pred[]{:T(512)S(6)} %eq.10), kind=kOutput, calls=%fused_computation.10 | convolution fusion | flops 404226048 | bytes 2490369 | tf_op jit(solution)/shard_map/dot_general | solution.py:18
  175.9 12.5 %collective-permute-done.12 = f32[256,512]{0,1:T(8,128)S(1)} collective-permute-done((f32[256,512]{0,1:T(8,128)S(1)}, f32[256,512]{0,1:T(8,128)S(1)}, u32[]{:S(2)}, u32[]{:S(2)}) %collective-permute-start.12) | collective-permute-done | bytes 524320 | tf_op jit(solution)/shard_map/ppermute | solution.py:14
  190.8 22.0 %collective-permute-done.13 = f32[256,512]{0,1:T(8,128)S(1)} collective-permute-done((f32[256,512]{0,1:T(8,128)S(1)}, f32[256,512]{0,1:T(8,128)S(1)}, u32[]{:S(2)}, u32[]{:S(2)}) %collective-permute-start.13) | collective-permute-done | bytes 524320 | tf_op jit(solution)/shard_map/ppermute | solution.py:14
  217.2 3.6 %collective-permute-done.8 = f32[64,256]{1,0:T(8,128)S(1)} collective-permute-done((f32[64,256]{1,0:T(8,128)S(1)}, f32[64,256]{1,0:T(8,128)S(1)}, u32[]{:S(2)}, u32[]{:S(2)}) %collective-permute-start.8) | collective-permute-done | bytes 65568 | tf_op jit(solution)/shard_map/ppermute | solution.py:14
  222.9 6.1 %collective-permute-done.15 = f32[256,512]{0,1:T(8,128)S(1)} collective-permute-done((f32[256,512]{0,1:T(8,128)S(1)}, f32[256,512]{0,1:T(8,128)S(1)}, u32[]{:S(2)}, u32[]{:S(2)}) %collective-permute-start.15) | collective-permute-done | bytes 524320 | tf_op jit(solution)/shard_map/ppermute | solution.py:14
  236.3 3.2 %collective-permute-done.17 = f32[16,512]{1,0:T(8,128)S(1)} collective-permute-done((f32[16,512]{1,0:T(8,128)S(1)}, f32[16,512]{1,0:T(8,128)S(1)}, u32[]{:S(2)}, u32[]{:S(2)}) %collective-permute-start.17) | collective-permute-done | bytes 32800 | tf_op jit(solution)/shard_map/ppermute | solution.py:14
  248.5 5.8 %collective-permute-done.2 = f32[256,256]{1,0:T(8,128)S(1)} collective-permute-done((f32[256,256]{1,0:T(8,128)S(1)}, f32[256,256]{1,0:T(8,128)S(1)}, u32[]{:S(2)}, u32[]{:S(2)}) %collective-permute-start.2) | collective-permute-done | bytes 262176 | tf_op jit(solution)/shard_map/ppermute | solution.py:14
  264.9 5.4 %collective-permute-done.21 = f32[64,512]{1,0:T(8,128)S(1)} collective-permute-done((f32[64,512]{1,0:T(8,128)S(1)}, f32[64,512]{1,0:T(8,128)S(1)}, u32[]{:S(2)}, u32[]{:S(2)}) %collective-permute-start.21) | collective-permute-done | bytes 131104 | tf_op jit(solution)/shard_map/ppermute | solution.py:14
  272.8 13.5 %collective-permute-done.3 = f32[512,256]{1,0:T(8,128)S(1)} collective-permute-done((f32[512,256]{1,0:T(8,128)S(1)}, f32[512,256]{1,0:T(8,128)S(1)}, u32[]{:S(2)}, u32[]{:S(2)}) %collective-permute-start.3) | collective-permute-done | bytes 524320 | tf_op jit(solution)/shard_map/ppermute | solution.py:14
  286.2 5.0 %collective-permute-done.22 = f32[128,512]{1,0:T(8,128)S(1)} collective-permute-done((f32[128,512]{1,0:T(8,128)S(1)}, f32[128,512]{1,0:T(8,128)S(1)}, u32[]{:S(2)}, u32[]{:S(2)}) %collective-permute-start.22) | collective-permute-done | bytes 262176 | tf_op jit(solution)/shard_map/ppermute | solution.py:14
  293.2 3.5 %convolution_subtract_fusion = f32[512,256]{1,0:T(8,128)S(1)} fusion(f32[512,256]{1,0:T(8,128)S(1)} %copy-done.6, f32[1024,512]{1,0:T(8,128)S(1)} %fusion.13, f32[256,1024]{1,0:T(8,128)S(1)} %copy-done.8), kind=kOutput, calls=%fused_computation.17 | convolution fusion | flops 1610743808 | bytes 4194304 | tf_op jit(solution)/shard_map/dot_general | solution.py:18
  298.6 8.6 %subtract_bitcast_fusion = f32[1024,512]{0,1:T(8,128)} fusion(f32[512,1024]{1,0:T(8,128)S(1)} %copy-done.2, f32[512,1024]{1,0:T(8,128)S(1)} %fusion.49, f32[1024,1024]{1,0:T(8,128)S(1)} %copy-done.3), kind=kOutput, calls=%fused_computation.16 | convolution fusion | flops 6442975232 | bytes 10485760 | tf_op jit(solution)/shard_map/dot_general | solution.py:18
  307.2 2.9 copy.11
  310.1 6.9 %scatter_custom_fusion = f32[1024,512]{1,0:T(8,128)} fusion(s32[1024]{0:T(1024)S(1)} %bitcast.35, f32[1024,512]{1,0:T(8,128)} %copy.11, f32[]{:T(128)} %constant.12.clone.1), kind=kCustom, calls=%fused_computation.40 | custom fusion | bytes 2097664 | tf_op jit(solution)/shard_map/scatter | solution.py:102
  (80 shorter events, 64.0 us)
Async XLA Ops:
  26.8 15.3 %collective-permute-start = (f32[256,512]{1,0:T(8,128)}, f32[256,512]{1,0:T(8,128)}, u32[]{:S(2)}, u32[]{:S(2)}) collective-permute-start(f32[256,512]{1,0:T(8,128)} %convolution_bitcast_fusion.2), channel_id=1, source_target_pairs={{0,1},{1,0},{2,3},{3,2},{4,5},{5,4},{6,7},{7,6},{8,9},{9,8},{10,11... | collective-permute-start | bytes 1572872 | tf_op jit(solution)/shard_map/ppermute | solution.py:14
  44.8 48.0 %collective-permute-start.1 = (f32[512,512]{1,0:T(8,128)}, f32[512,512]{1,0:T(8,128)}, u32[]{:S(2)}, u32[]{:S(2)}) collective-permute-start(f32[512,512]{1,0:T(8,128)} %maximum_select_fusion.4), channel_id=1, source_target_pairs={{0,2},{2,0},{1,3},{3,1},{4,6},{6,4},{5,7},{7,5},{8,10},{10,8},{9,1... | collective-permute-start | bytes 3145736 | tf_op jit(solution)/shard_map/ppermute | solution.py:14
  47.5 51.2 %copy-start.7 = (f32[256,256]{1,0:T(8,128)S(1)}, f32[256,256]{1,0:T(8,128)}, u32[]{:S(2)}) copy-start(f32[256,256]{1,0:T(8,128)} %param.14) | copy-start | bytes 786436
  99.4 13.0 %collective-permute-start.4 = (f32[256,512]{1,0:T(8,128)S(1)}, f32[256,512]{1,0:T(8,128)S(1)}, u32[]{:S(2)}, u32[]{:S(2)}) collective-permute-start(f32[256,512]{1,0:T(8,128)S(1)} %convolution_bitcast_fusion.1), channel_id=1, source_target_pairs={{0,1},{1,0},{2,3},{3,2},{4,5},{5,4},{6,7},{7,6},{8,9},{9,8},{10,11... | collective-permute-start | bytes 1572872 | tf_op jit(solution)/shard_map/ppermute | solution.py:14
  112.5 26.0 %collective-permute-start.5 = (f32[256,512]{1,0:T(8,128)S(1)}, f32[256,512]{1,0:T(8,128)S(1)}, u32[]{:S(2)}, u32[]{:S(2)}) collective-permute-start(f32[256,512]{1,0:T(8,128)S(1)} %add.46), channel_id=1, source_target_pairs={{0,2},{2,0},{1,3},{3,1},{4,6},{6,4},{5,7},{7,5},{8,10},{10,8},{9,1... | collective-permute-start | bytes 1572872 | tf_op jit(solution)/shard_map/ppermute | solution.py:14
  139.3 2.3 collective-permute-start.6
  144.3 25.5 %collective-permute-start.7 = (f32[512,512]{1,0:T(8,128)}, f32[512,512]{1,0:T(8,128)}, u32[]{:S(2)}, u32[]{:S(2)}) collective-permute-start(f32[512,512]{1,0:T(8,128)} %maximum_select_fusion.7), channel_id=1, source_target_pairs={{0,8},{8,0},{1,9},{9,1},{2,10},{10,2},{3,11},{11,3},{4,12},{12,4},... | collective-permute-start | bytes 3145736 | tf_op jit(solution)/shard_map/ppermute | solution.py:14
  175.2 13.2 %collective-permute-start.12 = (f32[256,512]{0,1:T(8,128)S(1)}, f32[256,512]{0,1:T(8,128)S(1)}, u32[]{:S(2)}, u32[]{:S(2)}) collective-permute-start(f32[256,512]{0,1:T(8,128)S(1)} %convolution_bitcast_fusion), channel_id=1, source_target_pairs={{0,1},{1,0},{2,3},{3,2},{4,5},{5,4},{6,7},{7,6},{8,9},{9,8},{10,11... | collective-permute-start | bytes 1572872 | tf_op jit(solution)/shard_map/ppermute | solution.py:14
  188.4 24.4 %collective-permute-start.13 = (f32[256,512]{0,1:T(8,128)S(1)}, f32[256,512]{0,1:T(8,128)S(1)}, u32[]{:S(2)}, u32[]{:S(2)}) collective-permute-start(f32[256,512]{0,1:T(8,128)S(1)} %add.48), channel_id=1, source_target_pairs={{0,2},{2,0},{1,3},{3,1},{4,6},{6,4},{5,7},{7,5},{8,10},{10,8},{9,1... | collective-permute-start | bytes 1572872 | tf_op jit(solution)/shard_map/ppermute | solution.py:14
  212.9 2.0 collective-permute-start.14
  215.0 14.0 %collective-permute-start.15 = (f32[256,512]{0,1:T(8,128)S(1)}, f32[256,512]{0,1:T(8,128)S(1)}, u32[]{:S(2)}, u32[]{:S(2)}) collective-permute-start(f32[256,512]{0,1:T(8,128)S(1)} %add.50), channel_id=1, source_target_pairs={{0,8},{8,0},{1,9},{9,1},{2,10},{10,2},{3,11},{11,3},{4,12},{12,4},... | collective-permute-start | bytes 1572872 | tf_op jit(solution)/shard_map/ppermute | solution.py:14
  216.5 4.3 %collective-permute-start.8 = (f32[64,256]{1,0:T(8,128)S(1)}, f32[64,256]{1,0:T(8,128)S(1)}, u32[]{:S(2)}, u32[]{:S(2)}) collective-permute-start(f32[64,256]{1,0:T(8,128)S(1)} %copy-done.10), channel_id=1, source_target_pairs={{0,1},{1,0},{2,3},{3,2},{4,5},{5,4},{6,7},{7,6},{8,9},{9,8},{10,11... | collective-permute-start | bytes 196616 | tf_op jit(solution)/shard_map/ppermute | solution.py:14
  220.8 11.0 %collective-permute-start.9 = (f32[128,256]{1,0:T(8,128)S(1)}, f32[128,256]{1,0:T(8,128)S(1)}, u32[]{:S(2)}, u32[]{:S(2)}) collective-permute-start(f32[128,256]{1,0:T(8,128)S(1)} %maximum_select_fusion.19), channel_id=1, source_target_pairs={{0,2},{2,0},{1,3},{3,1},{4,6},{6,4},{5,7},{7,5},{8,10},{10,8},{9,1... | collective-permute-start | bytes 393224 | tf_op jit(solution)/shard_map/ppermute | solution.py:14
  230.3 4.6 %collective-permute-start.16 = (f32[32,512]{1,0:T(8,128)}, f32[32,512]{1,0:T(8,128)}, u32[]{:S(2)}, u32[]{:S(2)}) collective-permute-start(f32[32,512]{1,0:T(8,128)} %convolution_bitcast_fusion.3), channel_id=1, source_target_pairs={{0,16},{16,0},{1,17},{17,1},{2,18},{18,2},{3,19},{19,3},{4,20},{20... | collective-permute-start | bytes 196616 | tf_op jit(solution)/shard_map/ppermute | solution.py:14
  232.5 9.2 %collective-permute-start.10 = (f32[256,256]{1,0:T(8,128)}, f32[256,256]{1,0:T(8,128)}, u32[]{:S(2)}, u32[]{:S(2)}) collective-permute-start(f32[256,256]{1,0:T(8,128)} %maximum_select_fusion.16), channel_id=1, source_target_pairs={{0,4},{4,0},{1,5},{5,1},{2,6},{6,2},{3,7},{7,3},{8,12},{12,8},{9,1... | collective-permute-start | bytes 786440 | tf_op jit(solution)/shard_map/ppermute | solution.py:14
  235.6 3.9 %collective-permute-start.17 = (f32[16,512]{1,0:T(8,128)S(1)}, f32[16,512]{1,0:T(8,128)S(1)}, u32[]{:S(2)}, u32[]{:S(2)}) collective-permute-start(f32[16,512]{1,0:T(8,128)S(1)} %dynamic-slice_add_fusion), channel_id=1, source_target_pairs={{0,1},{1,0},{2,3},{3,2},{4,5},{5,4},{6,7},{7,6},{8,9},{9,8},{10,11... | collective-permute-start | bytes 98312 | tf_op jit(solution)/shard_map/ppermute | solution.py:14
  239.6 5.9 %collective-permute-start.18 = (f32[32,512]{1,0:T(8,128)S(1)}, f32[32,512]{1,0:T(8,128)S(1)}, u32[]{:S(2)}, u32[]{:S(2)}) collective-permute-start(f32[32,512]{1,0:T(8,128)S(1)} %maximum_select_fusion.21), channel_id=1, source_target_pairs={{0,2},{2,0},{1,3},{3,1},{4,6},{6,4},{5,7},{7,5},{8,10},{10,8},{9,1... | collective-permute-start | bytes 196616 | tf_op jit(solution)/shard_map/ppermute | solution.py:14
  242.9 13.7 %collective-permute-start.11 = (f32[512,256]{1,0:T(8,128)S(1)}, f32[512,256]{1,0:T(8,128)S(1)}, u32[]{:S(2)}, u32[]{:S(2)}) collective-permute-start(f32[512,256]{1,0:T(8,128)S(1)} %maximum_select_fusion.11), channel_id=1, source_target_pairs={{0,8},{8,0},{1,9},{9,1},{2,10},{10,2},{3,11},{11,3},{4,12},{12,4},... | collective-permute-start | bytes 1572872 | tf_op jit(solution)/shard_map/ppermute | solution.py:14
  245.5 1.4 collective-permute-start.19
  245.6 8.7 %collective-permute-start.2 = (f32[256,256]{1,0:T(8,128)S(1)}, f32[256,256]{1,0:T(8,128)S(1)}, u32[]{:S(2)}, u32[]{:S(2)}) collective-permute-start(f32[256,256]{1,0:T(8,128)S(1)} %copy-done.7), channel_id=1, source_target_pairs={{0,1},{1,0},{2,3},{3,2},{4,5},{5,4},{6,7},{7,6},{8,9},{9,8},{10,11... | collective-permute-start | bytes 786440 | tf_op jit(solution)/shard_map/ppermute | solution.py:14
  246.9 12.5 %collective-permute-start.20 = (f32[128,512]{1,0:T(8,128)S(1)}, f32[128,512]{1,0:T(8,128)S(1)}, u32[]{:S(2)}, u32[]{:S(2)}) collective-permute-start(f32[128,512]{1,0:T(8,128)S(1)} %maximum_select_fusion.17), channel_id=1, source_target_pairs={{0,8},{8,0},{1,9},{9,1},{2,10},{10,2},{3,11},{11,3},{4,12},{12,4},... | collective-permute-start | bytes 786440 | tf_op jit(solution)/shard_map/ppermute | solution.py:14
  254.4 31.9 %collective-permute-start.3 = (f32[512,256]{1,0:T(8,128)S(1)}, f32[512,256]{1,0:T(8,128)S(1)}, u32[]{:S(2)}, u32[]{:S(2)}) collective-permute-start(f32[512,256]{1,0:T(8,128)S(1)} %maximum_select_fusion.10), channel_id=1, source_target_pairs={{0,2},{2,0},{1,3},{3,1},{4,6},{6,4},{5,7},{7,5},{8,10},{10,8},{9,1... | collective-permute-start | bytes 1572872 | tf_op jit(solution)/shard_map/ppermute | solution.py:14
  263.1 7.2 %collective-permute-start.21 = (f32[64,512]{1,0:T(8,128)S(1)}, f32[64,512]{1,0:T(8,128)S(1)}, u32[]{:S(2)}, u32[]{:S(2)}) collective-permute-start(f32[64,512]{1,0:T(8,128)S(1)} %fusion.12), channel_id=1, source_target_pairs={{0,1},{1,0},{2,3},{3,2},{4,5},{5,4},{6,7},{7,6},{8,9},{9,8},{10,11... | collective-permute-start | bytes 393224 | tf_op jit(solution)/shard_map/ppermute | solution.py:14
  270.3 21.0 %collective-permute-start.22 = (f32[128,512]{1,0:T(8,128)S(1)}, f32[128,512]{1,0:T(8,128)S(1)}, u32[]{:S(2)}, u32[]{:S(2)}) collective-permute-start(f32[128,512]{1,0:T(8,128)S(1)} %maximum_select_fusion.18), channel_id=1, source_target_pairs={{0,2},{2,0},{1,3},{3,1},{4,6},{6,4},{5,7},{7,5},{8,10},{10,8},{9,1... | collective-permute-start | bytes 786440 | tf_op jit(solution)/shard_map/ppermute | solution.py:14
  (11 other events, 217.8 us)
where the time goes:
time: 323 us; the launch traced here: 317 us
  waiting for transfers between devices  205 us (63%)
  matrix products  51.6 us (16%)
  starting transfers between devices  33.2 us (10%)
  local copies, waits for them, and re-layouts  16.8 us (5%)
  other arithmetic  10.3 us (3%)
    ppermute x23, waiting for transfers between devices, from_partner(): return lax.ppermute(block, axis, route)  205 us
    dot_general x10, matrix products, matmul(): return jnp.dot(left, right, precision=lax.Precision.HIGHEST)  46.6 us
    ppermute x23, starting transfers between devices, from_partner(): return lax.ppermute(block, axis, route)  33.2 us
    select_n x10, other arithmetic, doubling(): jnp.where(upper, jnp.concatenate([other, block], axis_dim), jnp.concatena...  7.49 us
    scatter x1, local copies, waits for them, and re-layouts, per_device(): return jnp.zeros_like(tree_order).at[order_row].set(tree_order)  6.86 us
  transfers between devices with their start and end apart: 23, of which 21 were waited for; matrix products, arithmetic and copies ran while one was open for 2% of the time, Pallas kernels for 0%

commit v1 on v0

v1 whole, which is shorter than its diff:
```python
import functools

import jax
import jax.numpy as jnp
from jax import lax
from jax.experimental import pallas as pl
from jax.experimental.pallas import tpu as pltpu
from jax.sharding import PartitionSpec as P

F32 = jnp.float32
BF16 = jnp.bfloat16
FAN = 4


def split(x):
    high = x.astype(BF16)
    return high, (x - high.astype(F32)).astype(BF16)


def dot(left, right):
    return jnp.dot(left, right, preferred_element_type=F32)


def dot3(left, right):
    return dot(left[0], right[0]) + (dot(left[0], right[1]) + dot(left[1], right[0]))


def matmul(left, right):
    return dot3(split(left), split(right))


def flat(block):
    return block.reshape(-1, block.shape[-1])


def kernel(
    depth,
    groups,
    tile,
    labels,
    order,
    inverse,
    basis,
    couple_one,
    transfer_one,
    couple_two,
    transfer_two,
    couple_top,
    placed_out,
    spread_out,
    block_out,
    lab_high,
    lab_low,
    sol_high,
    sol_low,
    column,
    proj_all,
    trans_one_all,
    couple_two_all,
    fixed_two_all,
    reduce_part,
    reduce_in,
    stack_two,
    trans_two_all,
    top_part,
    top_in,
    top_all,
    block_two,
    top_rows,
    solve_one,
    gain_one,
    line_send,
    line_recv,
    row_send,
    row_recv,
    quad_send,
    quad_recv,
    wide_send,
    wide_recv,
    tops_send,
    tops_recv,
):
    index = lax.axis_index("gx") * depth + lax.axis_index("gy")
    r = index % FAN
    sid = index // FAN
    q = sid % FAN
    g = sid // FAN
    wide = FAN * groups
    leaf, cols = labels.shape
    rank = basis.shape[1]
    part_cols = cols // FAN
    part_rows = rank // FAN
    slice_rows = couple_top.shape[0] // groups

    def device(sid_of, r_of):
        place = sid_of * FAN + r_of
        return (place // depth, place % depth)

    def copy(source, target, send, recv, where):
        return pltpu.make_async_remote_copy(
            src_ref=source,
            dst_ref=target,
            send_sem=send,
            recv_sem=recv,
            device_id=where,
            device_id_type=pl.DeviceIdType.MESH,
        )

    def line_copy(buf, which, way, step):
        slot = r - step if way == 0 else r + step
        to = r + 1 if way == 0 else r - 1
        slot = jnp.clip(slot, 0, FAN - 1)
        to = jnp.clip(to, 0, FAN - 1)
        return copy(
            buf.at[slot],
            buf.at[slot],
            line_send.at[which, way, step],
            line_recv.at[which, way, step],
            device(sid, to),
        )

    def sends(way, step):
        if way == 0:
            return jnp.logical_and(r >= step, r < FAN - 1)
        return jnp.logical_and(r + step <= FAN - 1, r > 0)

    def receives(way, step):
        if way == 0:
            return r - 1 - step >= 0
        return r + 1 + step <= FAN - 1

    def line_start(buf, which, step):
        for way in range(2):
            @pl.when(sends(way, step))
            def _():
                line_copy(buf, which, way, step).start()

    def line_wait(buf, which, step):
        for way in range(2):
            @pl.when(receives(way, step))
            def _():
                slot = r - 1 - step if way == 0 else r + 1 + step
                slot = jnp.clip(slot, 0, FAN - 1)
                copy(
                    buf.at[slot],
                    buf.at[slot],
                    line_send.at[which, way, step],
                    line_recv.at[which, way, step],
                    device(sid, (r + 1) % FAN),
                ).wait_recv()

    def line_finish(buf, which):
        for step in range(FAN - 1):
            for way in range(2):
                @pl.when(sends(way, step))
                def _():
                    line_copy(buf, which, way, step).wait_send()

    def over_row(which, source, target, step):
        return copy(
            source, target, row_send.at[which, step - 1], row_recv.at[which, step - 1],
            device(sid, (r + step) % FAN),
        )

    def over_quad(which, source, target, step):
        return copy(
            source, target, quad_send.at[which, step - 1], quad_recv.at[which, step - 1],
            device(g * FAN + (q + step) % FAN, r),
        )

    def over_wide(source, target, step):
        return copy(
            source, target, wide_send.at[step - 1], wide_recv.at[step - 1],
            device((sid + step) % wide, r),
        )

    def over_tops(source, target, step):
        return copy(
            source, target, tops_send.at[step - 1], tops_recv.at[step - 1],
            device((g + step) % groups * FAN + q, r),
        )

    barrier = pltpu.get_barrier_semaphore()
    for step in range(1, FAN):
        pl.semaphore_signal(
            barrier, inc=1, device_id=device(sid, (r + step) % FAN),
            device_id_type=pl.DeviceIdType.MESH,
        )
    for step in range(1, wide):
        pl.semaphore_signal(
            barrier, inc=1, device_id=device((sid + step) % wide, r),
            device_id_type=pl.DeviceIdType.MESH,
        )
    pl.semaphore_wait(barrier, FAN - 1 + wide - 1)

    couple_two_all[r] = couple_two[...]
    trans_one_all[r] = transfer_one[...]
    trans_two_all[q, r] = transfer_two[...]
    top_rows[r, g] = couple_top[pl.ds(pl.multiple_of(g * slice_rows, slice_rows), slice_rows), :]
    line_start(couple_two_all, 1, 0)
    row_two = [
        over_row(0, trans_two_all.at[q, r], trans_two_all.at[q, r], s) for s in range(1, FAN)
    ]
    for c in row_two:
        c.start()
    tops = []
    for s in range(1, groups):
        other = (g + s) % groups
        tops.append(
            over_tops(
                couple_top.at[pl.ds(pl.multiple_of(other * slice_rows, slice_rows), slice_rows)],
                top_rows.at[r, g],
                s,
            )
        )
        tops[-1].start()

    lab_high[...], lab_low[...] = split(labels[...])
    position = jnp.broadcast_to(order[...].astype(F32), (128, leaf)).T
    column[...] = position.astype(jnp.int32)
    rhs_high, rhs_low = placed_high, placed_low = sol_high.at[0], sol_low.at[0]
    sol_h, sol_l = sol_high.at[1], sol_low.at[1]
    tiles = leaf // tile

    def rows_of(step):
        return pl.ds(pl.multiple_of(step * tile, tile), tile)

    @pl.loop(0, tiles)
    def _(step):
        rows = rows_of(step)
        hot = column[rows, 0:1] == lax.broadcasted_iota(jnp.int32, (tile, leaf), 1)
        hot = hot.astype(F32).astype(BF16)
        rhs_high[rows, :] = dot(hot, lab_high[...]).astype(BF16)
        rhs_low[rows, :] = dot(hot, lab_low[...]).astype(BF16)

    @pl.loop(0, tiles)
    def _(step):
        rows = rows_of(step)
        value = dot3(split(inverse[rows, :]), (rhs_high[...], rhs_low[...]))
        sol_h[rows, :], sol_l[rows, :] = split(value)

    proj_all[r] = dot3(split(basis[...].T), (sol_h[...], sol_l[...]))
    line_start(proj_all, 0, 0)

    basis_parts = split(basis[...])
    lab_high[:, :rank], lab_low[:, :rank] = basis_parts

    @pl.loop(0, tiles)
    def _(step):
        rows = rows_of(step)
        value = dot3(split(inverse[rows, :]), (lab_high[:, :rank], lab_low[:, :rank]))
        rhs_high[rows, :rank], rhs_low[rows, :rank] = split(value)

    line_wait(proj_all, 0, 0)
    line_start(proj_all, 0, 1)

    @pl.loop(0, tiles)
    def _(step):
        rows = rows_of(step)
        hot = (lax.broadcasted_iota(jnp.int32, (tile, leaf), 0) + step * tile) == order[...]
        hot = hot.astype(F32).astype(BF16)
        placed_out[rows, :] = dot(hot, sol_h[...]) + dot(hot, sol_l[...])
        spread_out[rows, :] = dot(hot, rhs_high[:, :rank]) + dot(hot, rhs_low[:, :rank])

    for c in row_two:
        c.wait_recv()
    for c in tops:
        c.wait_recv()
    quad_two = [
        over_quad(0, trans_two_all.at[q], trans_two_all.at[q], s) for s in range(1, FAN)
    ]
    row_top = [over_row(1, top_rows.at[r], top_rows.at[r], s) for s in range(1, FAN)]
    for c in quad_two + row_top:
        c.start()

    line_wait(proj_all, 0, 1)
    line_start(proj_all, 0, 2)
    line_wait(couple_two_all, 1, 0)
    line_start(couple_two_all, 1, 1)
    line_wait(proj_all, 0, 2)

    solve_one[...] = matmul(couple_one[...], flat(proj_all[...]))
    reduced = matmul(transfer_one[...].T, solve_one[...])
    for part in range(FAN):
        reduce_part[part] = reduced[:, part * part_cols : (part + 1) * part_cols]
    row_reduce = [
        over_row(2, reduce_part.at[(r + s) % FAN], reduce_in.at[s - 1], s) for s in range(1, FAN)
    ]
    for c in row_reduce:
        c.start()
    line_wait(couple_two_all, 1, 1)
    line_start(couple_two_all, 1, 2)
    line_start(trans_one_all, 2, 0)
    for c in row_reduce:
        c.wait_recv()
    stack_two[q] = reduce_part[r] + reduce_in[0] + (reduce_in[1] + reduce_in[2])
    quad_stack = [over_quad(1, stack_two.at[q], stack_two.at[q], s) for s in range(1, FAN)]
    for c in quad_stack:
        c.start()
    for c in quad_two + row_top:
        c.wait_recv()
    line_wait(couple_two_all, 1, 2)
    line_wait(trans_one_all, 2, 0)
    line_start(trans_one_all, 2, 1)

    couple = split(flat(couple_two_all[...]))
    gain_two = split(dot3(couple, split(flat(trans_two_all[...]))))
    own_two = flat(trans_two_all[q]).T
    for c in quad_stack:
        c.wait_recv()
    solve_two = dot3(couple, split(flat(stack_two[...])))
    top_part[...] = matmul(own_two, solve_two).reshape(FAN, part_rows, part_cols)
    quad_reduce = [
        over_quad(2, top_part.at[(q + s) % FAN], top_in.at[s - 1], s) for s in range(1, FAN)
    ]
    for c in quad_reduce:
        c.start()
    for c in quad_reduce:
        c.wait_recv()
    top_all[sid] = top_part[q] + top_in[0] + (top_in[1] + top_in[2])
    wide_top = [over_wide(top_all.at[sid], top_all.at[sid], s) for s in range(1, wide)]
    for c in wide_top:
        c.start()
    for c in wide_top:
        c.wait_recv()
    total = jnp.zeros((part_rows, part_cols), F32)
    for other in range(groups):
        total = total + matmul(
            flat(top_rows[:, other]), flat(top_all[other * FAN : (other + 1) * FAN])
        )
    block_two[q] = total
    quad_block = [over_quad(3, block_two.at[q], block_two.at[q], s) for s in range(1, FAN)]
    for c in quad_block:
        c.start()
    for c in quad_block:
        c.wait_recv()
    fixed_two_all[r] = solve_two - dot3(gain_two, split(flat(block_two[...])))
    line_start(fixed_two_all, 3, 0)
    line_wait(trans_one_all, 2, 1)
    line_start(trans_one_all, 2, 2)
    line_wait(fixed_two_all, 3, 0)
    line_start(fixed_two_all, 3, 1)
    line_wait(trans_one_all, 2, 2)
    gain_one[...] = matmul(couple_one[...], flat(trans_one_all[...]))
    line_wait(fixed_two_all, 3, 1)
    line_start(fixed_two_all, 3, 2)
    line_wait(fixed_two_all, 3, 2)
    gain = split(gain_one[...])
    for part in range(FAN):
        here = slice(part * part_cols, (part + 1) * part_cols)
        block_out[:, here] = solve_one[:, here] - dot3(gain, split(fixed_two_all[part]))

    for which, buf in enumerate((proj_all, couple_two_all, trans_one_all, fixed_two_all)):
        line_finish(buf, which)
    for c in (
        row_two + tops + quad_two + row_top + row_reduce + quad_stack + quad_reduce
        + wide_top + quad_block
    ):
        c.wait_send()


def last(placed, spread, block, out):
    out[...] = placed[...] - matmul(spread[...], block[...])


def per_device(
    depth,
    groups,
    labels,
    point_order,
    leaf_inverse,
    leaf_basis,
    couple_one,
    transfer_one,
    couple_two,
    transfer_two,
    couple_top,
):
    leaf, cols = labels.shape
    rank = leaf_basis.shape[1]
    part_cols = cols // FAN
    part_rows = rank // FAN
    slice_rows = couple_top.shape[0] // groups
    wide = FAN * groups
    vmem = pl.BlockSpec(memory_space=pltpu.VMEM)
    dma = pltpu.SemaphoreType.DMA
    args = (
        labels, point_order, leaf_inverse, leaf_basis, couple_one, transfer_one,
        couple_two, transfer_two, couple_top,
    )
    placed, spread, block = pl.pallas_call(
        functools.partial(kernel, depth, groups, leaf // 4),
        out_shape=(
            jax.ShapeDtypeStruct((leaf, cols), F32),
            jax.ShapeDtypeStruct((leaf, rank), F32),
            jax.ShapeDtypeStruct((rank, cols), F32),
        ),
        in_specs=[vmem] * len(args),
        out_specs=(vmem, vmem, vmem),
        scratch_shapes=[
            pltpu.VMEM((leaf, cols), BF16),
            pltpu.VMEM((leaf, cols), BF16),
            pltpu.VMEM((2, leaf, cols), BF16),
            pltpu.VMEM((2, leaf, cols), BF16),
            pltpu.VMEM((leaf, 128), jnp.int32),
            pltpu.VMEM((FAN, rank, cols), F32),
            pltpu.VMEM((FAN, *transfer_one.shape), F32),
            pltpu.VMEM((FAN, *couple_two.shape), F32),
            pltpu.VMEM((FAN, rank, part_cols), F32),
            pltpu.VMEM((FAN, rank, part_cols), F32),
            pltpu.VMEM((FAN - 1, rank, part_cols), F32),
            pltpu.VMEM((FAN, rank, part_cols), F32),
            pltpu.VMEM((FAN, FAN, *transfer_two.shape), F32),
            pltpu.VMEM((FAN, part_rows, part_cols), F32),
            pltpu.VMEM((FAN - 1, part_rows, part_cols), F32),
            pltpu.VMEM((wide, part_rows, part_cols), F32),
            pltpu.VMEM((FAN, part_rows, part_cols), F32),
            pltpu.VMEM((FAN, groups, slice_rows, rank), F32),
            pltpu.VMEM((rank, cols), F32),
            pltpu.VMEM((rank, rank), F32),
            dma((4, 2, FAN - 1)),
            dma((4, 2, FAN - 1)),
            dma((3, FAN - 1)),
            dma((3, FAN - 1)),
            dma((4, FAN - 1)),
            dma((4, FAN - 1)),
            dma((wide - 1,)),
            dma((wide - 1,)),
            dma((max(groups - 1, 1),)),
            dma((max(groups - 1, 1),)),
        ],
        compiler_params=pltpu.CompilerParams(
            collective_id=0, has_side_effects=True, vmem_limit_bytes=56 * 1024 * 1024
        ),
    )(*args)
    tile = leaf // 4
    return pl.pallas_call(
        last,
        out_shape=jax.ShapeDtypeStruct((leaf, cols), F32),
        grid=(leaf // tile,),
        in_specs=[
            pl.BlockSpec((tile, cols), lambda i: (i, 0)),
            pl.BlockSpec((tile, rank), lambda i: (i, 0)),
            pl.BlockSpec((rank, cols), lambda i: (0, 0)),
        ],
        out_specs=pl.BlockSpec((tile, cols), lambda i: (i, 0)),
        compiler_params=pltpu.CompilerParams(vmem_limit_bytes=32 * 1024 * 1024),
    )(placed, spread, block)


def solution(mesh):
    depth = mesh.shape["gy"]
    groups = mesh.shape["gx"] * depth // (FAN * FAN)
    spec = P(("gx", "gy"), None)
    return jax.shard_map(
        functools.partial(per_device, depth, groups),
        mesh=mesh,
        in_specs=(spec,) * 9,
        out_specs=spec,
        check_vma=False,
    )
```

time: 323 us -> 125 us (0.39); the launches traced: 317 us -> 124 us
  waiting for transfers between devices: 205 us -> 0 us
  Pallas kernels: 0 us -> 121 us
  matrix products: 51.6 us -> 0 us
  starting transfers between devices: 33.2 us -> 0 us
  local copies, waits for them, and re-layouts: 16.8 us -> 3.85 us
  other arithmetic: 10.3 us -> 0 us
    ppermute x23 -> x0, waiting for transfers between devices: 205 us -> none  [from_partner(): return lax.ppermute(block, axis, route)]
    pallas_call x0 -> x2, Pallas kernels: none -> 121 us  [the longest x1 118 us: per_device(): pl.pallas_call(functools.partial(kernel, depth, groups, leaf // 4), out_s...]
    dot_general x13 -> x0, matrix products: 51.6 us -> none  [the longest x10 46.6 us: matmul(): return jnp.dot(left, right, precision=lax.Precision.HIGHEST)]
    ppermute x23 -> x0, starting transfers between devices: 33.2 us -> none  [from_partner(): return lax.ppermute(block, axis, route)]
    select_n x11 -> x0, other arithmetic: 8.33 us -> none  [the longest x10 7.49 us: doubling(): jnp.where(upper, jnp.concatenate([other, block], axis_dim), jnp.concatena...]
    scatter x1 -> x0, local copies, waits for them, and re-layouts: 6.86 us -> none  [per_device(): return jnp.zeros_like(tree_order).at[order_row].set(tree_order)]
    gather x1 -> x0, local copies, waits for them, and re-layouts: 4.86 us -> none  [per_device(): rhs = labels[order_row]]
  transfers between devices with their start and end apart: 23 -> 0, of which waited for: 21 -> 0; matrix products, arithmetic and copies ran while one was open for 2% -> 0% of each run, Pallas kernels for 0% -> 0%
where the time goes in v1:
time: 125 us; the launch traced here: 124 us
  Pallas kernels  121 us (97%)
  local copies, waits for them, and re-layouts  3.85 us (3%)
    pallas_call x1, Pallas kernels, per_device(): pl.pallas_call(functools.partial(kernel, depth, groups, leaf // 4), out_s...  118 us
    unnamed x6, local copies, waits for them, and re-layouts  3.85 us
    pallas_call x1, Pallas kernels, per_device(): pl.pallas_call(last, out_shape=jax.ShapeDtypeStruct((leaf, cols), F32), g...  2.77 us

profile of v1, /device:TPU:0, one launch (start us, length us, event | category | flops | bytes accessed | tf_op | source)
XLA Modules:
  0.0 124.5 jit_solution(15409051059726850106)
XLA Ops:
  0.0 117.8 %shard_map.91 = (f32[1024,512]{1,0:T(8,128)}, f32[1024,256]{1,0:T(8,128)}, f32[256,512]{1,0:T(8,128)}) custom-call(f32[1024,512]{1,0:T(8,128)} %labels.1, s32[1,1024]{1,0:T(1,128)} %order.1, f32[1024,1024]{1,0:T(8,128)} %inverse.1, f32[1024,256]{1,0:T(8,128)} %basis.1, f32[256,1024]{1,0:T(8,128)} %couple_one.1, f32[256,256]{1,0:T(8,128)} %transfer_one.1, ...), custom_call_target="tpu_custom_call" | custom-call | tf_op jit(solution)/shard_map/pallas_call | solution.py:391
  117.8 0.0 copy-start
  117.9 1.6 %copy-done = f32[1024,512]{1,0:T(8,128)S(1)} copy-done((f32[1024,512]{1,0:T(8,128)S(1)}, f32[1024,512]{1,0:T(8,128)}, u32[]{:S(2)}) %copy-start) | copy-done | bytes 2097176
  119.4 0.0 copy-start.1
  119.4 1.2 copy-done.1
  120.7 0.0 copy-start.2
  120.7 1.0 copy-done.2
  121.7 2.8 %shard_map.92 = f32[1024,512]{1,0:T(8,128)} custom-call(f32[1024,512]{1,0:T(8,128)S(1)} %copy-done, f32[1024,256]{1,0:T(8,128)S(1)} %copy-done.1, f32[256,512]{1,0:T(8,128)S(1)} %copy-done.2), custom_call_target="tpu_custom_call" | custom-call | tf_op jit(solution)/shard_map/pallas_call | solution.py:437
Async XLA Ops:
  117.8 1.6 %copy-start = (f32[1024,512]{1,0:T(8,128)S(1)}, f32[1024,512]{1,0:T(8,128)}, u32[]{:S(2)}) copy-start(f32[1024,512]{1,0:T(8,128)} %get-tuple-element.8.placed) | copy-start | bytes 6291460
  119.4 1.2 copy-start.1
  120.7 1.0 copy-start.2

commit v2 on v1

--- a/solution.py
+++ b/solution.py
@@ -39,16 +39,19 @@
     tile,
     labels,
     order,
-    inverse,
+    inverse_hbm,
     basis,
     couple_one,
     transfer_one,
     couple_two,
     transfer_two,
     couple_top,
+    placed_hbm,
+    spread_hbm,
+    block_out,
     placed_out,
     spread_out,
-    block_out,
+    inverse,
     lab_high,
     lab_low,
     sol_high,
@@ -69,6 +72,13 @@
     top_rows,
     solve_one,
     gain_one,
+    couple_ward,
+    solve_ward,
+    gain_ward,
+    ward_part,
+    pair_send,
+    pair_recv,
+    local_sem,
     line_send,
     line_recv,
     row_send,
@@ -92,6 +102,10 @@
     part_rows = rank // FAN
     slice_rows = couple_top.shape[0] // groups
 
+    mate = r + 1 - 2 * (r % 2)
+    inner = jnp.logical_and(r > 0, r < FAN - 1)
+    outer = jnp.logical_not(inner)
+
     def device(sid_of, r_of):
         place = sid_of * FAN + r_of
         return (place // depth, place % depth)
@@ -168,6 +182,14 @@
             device(g * FAN + (q + step) % FAN, r),
         )
 
+    def to_mate(source, target, number):
+        return copy(source, target, pair_send.at[number], pair_recv.at[number], device(sid, mate))
+
+    def to_partner(source, target, number):
+        return copy(
+            source, target, pair_send.at[number], pair_recv.at[number], device(sid, FAN - 1 - r)
+        )
+
     def over_wide(source, target, step):
         return copy(
             source, target, wide_send.at[step - 1], wide_recv.at[step - 1],
@@ -193,16 +215,39 @@
         )
     pl.semaphore_wait(barrier, FAN - 1 + wide - 1)
 
-    couple_two_all[r] = couple_two[...]
+    proj_end = to_mate(proj_all.at[r], proj_all.at[r], 0)
+    proj_from = to_mate(proj_all.at[mate], proj_all.at[mate], 0)
+    couple_end = [
+        to_mate(couple_one.at[pl.ds(i * part_rows, part_rows)],
+                couple_ward.at[pl.ds(i * part_rows, part_rows)], 1 + i)
+        for i in range(FAN)
+    ]
+    trans_end = to_mate(trans_one_all.at[r], trans_one_all.at[r], 5)
+    trans_from = to_mate(trans_one_all.at[mate], trans_one_all.at[mate], 5)
+    proj_over = to_partner(proj_all.at[r], proj_all.at[r], 6)
+    proj_pass = to_partner(proj_all.at[mate], proj_all.at[mate], 7)
+    trans_over = to_partner(trans_one_all.at[r], trans_one_all.at[r], 8)
+    trans_pass = to_partner(trans_one_all.at[mate], trans_one_all.at[mate], 9)
+    reduce_over = to_partner(
+        reduce_part.at[pl.ds((1 - r // 2) * 2, 2)], reduce_in, 10
+    )
+    reduce_ward = to_mate(ward_part, stack_two.at[q], 11)
+    solve_back = to_mate(solve_ward, solve_one, 12)
+    gain_back = to_mate(gain_ward, gain_one, 13)
+
+    inverse_load = pltpu.make_async_copy(inverse_hbm, inverse, local_sem.at[0])
+    inverse_load.start()
+    width = couple_two.shape[1]
+    couple_two_all[r, :, :width] = couple_two[...]
+    couple_two_all[r, :, width:] = transfer_two[...]
     trans_one_all[r] = transfer_one[...]
-    trans_two_all[q, r] = transfer_two[...]
     top_rows[r, g] = couple_top[pl.ds(pl.multiple_of(g * slice_rows, slice_rows), slice_rows), :]
-    line_start(couple_two_all, 1, 0)
-    row_two = [
-        over_row(0, trans_two_all.at[q, r], trans_two_all.at[q, r], s) for s in range(1, FAN)
-    ]
-    for c in row_two:
-        c.start()
+    line_start(couple_two_all, 0, 0)
+
+    @pl.when(outer)
+    def _():
+        couple_end[0].start()
+
     tops = []
     for s in range(1, groups):
         other = (g + s) % groups
@@ -233,6 +278,8 @@
         rhs_high[rows, :] = dot(hot, lab_high[...]).astype(BF16)
         rhs_low[rows, :] = dot(hot, lab_low[...]).astype(BF16)
 
+    inverse_load.wait()
+
     @pl.loop(0, tiles)
     def _(step):
         rows = rows_of(step)
@@ -240,7 +287,14 @@
         sol_h[rows, :], sol_l[rows, :] = split(value)
 
     proj_all[r] = dot3(split(basis[...].T), (sol_h[...], sol_l[...]))
-    line_start(proj_all, 0, 0)
+
+    @pl.when(outer)
+    def _():
+        proj_end.start()
+
+    @pl.when(inner)
+    def _():
+        proj_over.start()
 
     basis_parts = split(basis[...])
     lab_high[:, :rank], lab_low[:, :rank] = basis_parts
@@ -251,8 +305,6 @@
         value = dot3(split(inverse[rows, :]), (lab_high[:, :rank], lab_low[:, :rank]))
         rhs_high[rows, :rank], rhs_low[rows, :rank] = split(value)
 
-    line_wait(proj_all, 0, 0)
-    line_start(proj_all, 0, 1)
 
     @pl.loop(0, tiles)
     def _(step):
@@ -262,49 +314,81 @@
         placed_out[rows, :] = dot(hot, sol_h[...]) + dot(hot, sol_l[...])
         spread_out[rows, :] = dot(hot, rhs_high[:, :rank]) + dot(hot, rhs_low[:, :rank])
 
-    for c in row_two:
-        c.wait_recv()
+    placed_store = pltpu.make_async_copy(placed_out, placed_hbm, local_sem.at[1])
+    spread_store = pltpu.make_async_copy(spread_out, spread_hbm, local_sem.at[2])
+    placed_store.start()
+    spread_store.start()
+
     for c in tops:
         c.wait_recv()
+    row_top = [over_row(0, top_rows.at[r], top_rows.at[r], s) for s in range(1, FAN)]
+
+    @pl.when(outer)
+    def _():
+        proj_end.wait_send()
+        for c in couple_end[1:]:
+            c.start()
+        trans_end.start()
+
+    @pl.when(inner)
+    def _():
+        proj_from.wait_recv()
+        proj_pass.start()
+        proj_over.wait_recv()
+        proj_pass.wait_recv()
+
+    line_wait(couple_two_all, 0, 0)
+    line_start(couple_two_all, 0, 1)
+    for c in row_top:
+        c.start()
+
+    @pl.when(inner)
+    def _():
+        stack_one = split(flat(proj_all[...]))
+        solve_one[...] = dot3(split(couple_one[...]), stack_one)
+        for c in couple_end:
+            c.wait_recv()
+        solve_ward[...] = dot3(split(couple_ward[...]), stack_one)
+        trans_from.wait_recv()
+        reduced = matmul(transfer_one[...].T, solve_one[...]) + matmul(
+            trans_one_all[mate].T, solve_ward[...]
+        )
+        for part in range(FAN):
+            reduce_part[part] = reduced[:, part * part_cols : (part + 1) * part_cols]
+        reduce_over.start()
+        reduce_over.wait_recv()
+        ward_part[...] = reduce_part[mate] + reduce_in[mate % 2]
+        reduce_ward.start()
+        stack_two[q] = reduce_part[r] + reduce_in[r % 2]
+
+    @pl.when(outer)
+    def _():
+        reduce_ward.wait_recv()
+
+    quad_stack = [over_quad(1, stack_two.at[q], stack_two.at[q], s) for s in range(1, FAN)]
+    for c in quad_stack:
+        c.start()
+
+    line_wait(couple_two_all, 0, 1)
+    line_start(couple_two_all, 0, 2)
+
+    @pl.when(inner)
+    def _():
+        solve_back.start()
+        trans_over.start()
+        trans_pass.start()
+
+    line_wait(couple_two_all, 0, 2)
+    trans_two_all[q] = couple_two_all[:, :, width:]
     quad_two = [
         over_quad(0, trans_two_all.at[q], trans_two_all.at[q], s) for s in range(1, FAN)
     ]
-    row_top = [over_row(1, top_rows.at[r], top_rows.at[r], s) for s in range(1, FAN)]
-    for c in quad_two + row_top:
+    for c in quad_two:
         c.start()
-
-    line_wait(proj_all, 0, 1)
-    line_start(proj_all, 0, 2)
-    line_wait(couple_two_all, 1, 0)
-    line_start(couple_two_all, 1, 1)
-    line_wait(proj_all, 0, 2)
-
-    solve_one[...] = matmul(couple_one[...], flat(proj_all[...]))
-    reduced = matmul(transfer_one[...].T, solve_one[...])
-    for part in range(FAN):
-        reduce_part[part] = reduced[:, part * part_cols : (part + 1) * part_cols]
-    row_reduce = [
-        over_row(2, reduce_part.at[(r + s) % FAN], reduce_in.at[s - 1], s) for s in range(1, FAN)
-    ]
-    for c in row_reduce:
-        c.start()
-    line_wait(couple_two_all, 1, 1)
-    line_start(couple_two_all, 1, 2)
-    line_start(trans_one_all, 2, 0)
-    for c in row_reduce:
-        c.wait_recv()
-    stack_two[q] = reduce_part[r] + reduce_in[0] + (reduce_in[1] + reduce_in[2])
-    quad_stack = [over_quad(1, stack_two.at[q], stack_two.at[q], s) for s in range(1, FAN)]
-    for c in quad_stack:
-        c.start()
-    for c in quad_two + row_top:
-        c.wait_recv()
-    line_wait(couple_two_all, 1, 2)
-    line_wait(trans_one_all, 2, 0)
-    line_start(trans_one_all, 2, 1)
-
-    couple = split(flat(couple_two_all[...]))
-    gain_two = split(dot3(couple, split(flat(trans_two_all[...]))))
+    for c in row_top:
+        c.wait_recv()
+
+    couple = split(flat(couple_two_all[:, :, :width]))
     own_two = flat(trans_two_all[q]).T
     for c in quad_stack:
         c.wait_recv()
@@ -315,6 +399,9 @@
     ]
     for c in quad_reduce:
         c.start()
+    for c in quad_two:
+        c.wait_recv()
+    gain_two = split(dot3(couple, split(flat(trans_two_all[...]))))
     for c in quad_reduce:
         c.wait_recv()
     top_all[sid] = top_part[q] + top_in[0] + (top_in[1] + top_in[2])
@@ -335,28 +422,54 @@
     for c in quad_block:
         c.wait_recv()
     fixed_two_all[r] = solve_two - dot3(gain_two, split(flat(block_two[...])))
-    line_start(fixed_two_all, 3, 0)
-    line_wait(trans_one_all, 2, 1)
-    line_start(trans_one_all, 2, 2)
-    line_wait(fixed_two_all, 3, 0)
-    line_start(fixed_two_all, 3, 1)
-    line_wait(trans_one_all, 2, 2)
-    gain_one[...] = matmul(couple_one[...], flat(trans_one_all[...]))
-    line_wait(fixed_two_all, 3, 1)
-    line_start(fixed_two_all, 3, 2)
-    line_wait(fixed_two_all, 3, 2)
+    line_start(fixed_two_all, 1, 0)
+
+    @pl.when(inner)
+    def _():
+        trans_over.wait_recv()
+        trans_pass.wait_recv()
+        trans_full = split(flat(trans_one_all[...]))
+        gain_ward[...] = dot3(split(couple_ward[...]), trans_full)
+        gain_back.start()
+        gain_one[...] = dot3(split(couple_one[...]), trans_full)
+
+    line_wait(fixed_two_all, 1, 0)
+    line_start(fixed_two_all, 1, 1)
+    line_wait(fixed_two_all, 1, 1)
+    line_start(fixed_two_all, 1, 2)
+    line_wait(fixed_two_all, 1, 2)
+
+    @pl.when(outer)
+    def _():
+        solve_back.wait_recv()
+        gain_back.wait_recv()
+
     gain = split(gain_one[...])
     for part in range(FAN):
         here = slice(part * part_cols, (part + 1) * part_cols)
         block_out[:, here] = solve_one[:, here] - dot3(gain, split(fixed_two_all[part]))
 
-    for which, buf in enumerate((proj_all, couple_two_all, trans_one_all, fixed_two_all)):
+    for which, buf in enumerate((couple_two_all, fixed_two_all)):
         line_finish(buf, which)
-    for c in (
-        row_two + tops + quad_two + row_top + row_reduce + quad_stack + quad_reduce
-        + wide_top + quad_block
-    ):
+
+    @pl.when(outer)
+    def _():
+        for c in couple_end:
+            c.wait_send()
+        trans_end.wait_send()
+
+    @pl.when(inner)
+    def _():
+        for c in (
+            proj_over, proj_pass, trans_over, trans_pass, reduce_over, reduce_ward,
+            solve_back, gain_back,
+        ):
+            c.wait_send()
+
+    for c in tops + row_top + quad_two + quad_stack + quad_reduce + wide_top + quad_block:
         c.wait_send()
+    placed_store.wait()
+    spread_store.wait()
 
 
 def last(placed, spread, block, out):
@@ -383,6 +496,7 @@
     slice_rows = couple_top.shape[0] // groups
     wide = FAN * groups
     vmem = pl.BlockSpec(memory_space=pltpu.VMEM)
+    far = pl.BlockSpec(memory_space=pl.ANY)
     dma = pltpu.SemaphoreType.DMA
     args = (
         labels, point_order, leaf_inverse, leaf_basis, couple_one, transfer_one,
@@ -395,9 +509,12 @@
             jax.ShapeDtypeStruct((leaf, rank), F32),
             jax.ShapeDtypeStruct((rank, cols), F32),
         ),
-        in_specs=[vmem] * len(args),
-        out_specs=(vmem, vmem, vmem),
+        in_specs=[vmem, vmem, far] + [vmem] * (len(args) - 3),
+        out_specs=(far, far, vmem),
         scratch_shapes=[
+            pltpu.VMEM((leaf, cols), F32),
+            pltpu.VMEM((leaf, rank), F32),
+            pltpu.VMEM((leaf, leaf), F32),
             pltpu.VMEM((leaf, cols), BF16),
             pltpu.VMEM((leaf, cols), BF16),
             pltpu.VMEM((2, leaf, cols), BF16),
@@ -405,10 +522,10 @@
             pltpu.VMEM((leaf, 128), jnp.int32),
             pltpu.VMEM((FAN, rank, cols), F32),
             pltpu.VMEM((FAN, *transfer_one.shape), F32),
-            pltpu.VMEM((FAN, *couple_two.shape), F32),
+            pltpu.VMEM((FAN, couple_two.shape[0], couple_two.shape[1] + rank), F32),
             pltpu.VMEM((FAN, rank, part_cols), F32),
             pltpu.VMEM((FAN, rank, part_cols), F32),
-            pltpu.VMEM((FAN - 1, rank, part_cols), F32),
+            pltpu.VMEM((2, rank, part_cols), F32),
             pltpu.VMEM((FAN, rank, part_cols), F32),
             pltpu.VMEM((FAN, FAN, *transfer_two.shape), F32),
             pltpu.VMEM((FAN, part_rows, part_cols), F32),
@@ -418,10 +535,17 @@
             pltpu.VMEM((FAN, groups, slice_rows, rank), F32),
             pltpu.VMEM((rank, cols), F32),
             pltpu.VMEM((rank, rank), F32),
-            dma((4, 2, FAN - 1)),
-            dma((4, 2, FAN - 1)),
-            dma((3, FAN - 1)),
-            dma((3, FAN - 1)),
+            pltpu.VMEM(couple_one.shape, F32),
+            pltpu.VMEM((rank, cols), F32),
+            pltpu.VMEM((rank, rank), F32),
+            pltpu.VMEM((rank, part_cols), F32),
+            dma((14,)),
+            dma((14,)),
+            dma((3,)),
+            dma((2, 2, FAN - 1)),
+            dma((2, 2, FAN - 1)),
+            dma((1, FAN - 1)),
+            dma((1, FAN - 1)),
             dma((4, FAN - 1)),
             dma((4, FAN - 1)),
             dma((wide - 1,)),
@@ -444,7 +568,7 @@
             pl.BlockSpec((rank, cols), lambda i: (0, 0)),
         ],
         out_specs=pl.BlockSpec((tile, cols), lambda i: (i, 0)),
-        compiler_params=pltpu.CompilerParams(vmem_limit_bytes=32 * 1024 * 1024),
+        compiler_params=pltpu.CompilerParams(vmem_limit_bytes=60 * 1024 * 1024),
     )(placed, spread, block)
 
 

time: 125 us -> 116 us (0.928)
  Pallas kernels: 121 us -> 116 us
  local copies, waits for them, and re-layouts: 3.85 us -> 0 us
    pallas_call x1, Pallas kernels: 118 us -> 111 us  [per_device(): pl.pallas_call(functools.partial(kernel, depth, groups, leaf // 4), out_s...]
    unnamed x6 -> x0, local copies, waits for them, and re-layouts: 3.85 us -> none
    pallas_call x1, Pallas kernels: 2.77 us -> 4.98 us  [per_device(): pl.pallas_call(last, out_shape=jax.ShapeDtypeStruct((leaf, cols), F32), g...]
where the time goes in v2:
time: 116 us
  Pallas kernels  116 us (100%)
    pallas_call x1, Pallas kernels, per_device(): pl.pallas_call(functools.partial(kernel, depth, groups, leaf // 4), out_s...  111 us
    pallas_call x1, Pallas kernels, per_device(): pl.pallas_call(last, out_shape=jax.ShapeDtypeStruct((leaf, cols), F32), g...  4.98 us

profile of v2, /device:TPU:0, one launch (start us, length us, event | category | flops | bytes accessed | tf_op | source)
XLA Modules:
  0.0 116.1 jit_solution(15512039430510867433)
XLA Ops:
  0.0 111.1 %shard_map.91 = (f32[1024,512]{1,0:T(8,128)}, f32[1024,256]{1,0:T(8,128)}, f32[256,512]{1,0:T(8,128)}) custom-call(f32[1024,512]{1,0:T(8,128)} %labels.1, s32[1,1024]{1,0:T(1,128)} %order.1, f32[1024,1024]{1,0:T(8,128)} %inverse_hbm.1, f32[1024,256]{1,0:T(8,128)} %basis.1, f32[256,1024]{1,0:T(8,128)} %couple_one.1, f32[256,256]{1,0:T(8,128)} %transfer_one.1, ...), custom_call_target="tpu_custom_call" | custom-call | tf_op jit(solution)/shard_map/pallas_call | solution.py:505
  111.1 5.0 %shard_map.92 = f32[1024,512]{1,0:T(8,128)} custom-call(f32[1024,512]{1,0:T(8,128)} %get-tuple-element.8.placed, f32[1024,256]{1,0:T(8,128)} %get-tuple-element.9.spread, f32[256,512]{1,0:T(8,128)} %get-tuple-element.10.block), custom_call_target="tpu_custom_call" | custom-call | tf_op jit(solution)/shard_map/pallas_call | solution.py:561

commit v3 on v2

--- a/solution.py
+++ b/solution.py
@@ -10,6 +10,7 @@
 F32 = jnp.float32
 BF16 = jnp.bfloat16
 FAN = 4
+TILES = 1
 
 
 def split(x):
@@ -235,6 +236,15 @@
     solve_back = to_mate(solve_ward, solve_one, 12)
     gain_back = to_mate(gain_ward, gain_one, 13)
 
+    two_end = to_mate(couple_two_all.at[r], couple_two_all.at[r], 14)
+    two_from = to_mate(couple_two_all.at[mate], couple_two_all.at[mate], 14)
+    two_over = to_partner(couple_two_all.at[r], couple_two_all.at[r], 15)
+    two_pass = to_partner(couple_two_all.at[mate], couple_two_all.at[mate], 16)
+    across, beyond = FAN - 1 - r, FAN - 1 - mate
+    two_own = to_mate(couple_two_all.at[r], couple_two_all.at[r], 17)
+    two_across = to_mate(couple_two_all.at[across], couple_two_all.at[across], 18)
+    two_beyond = to_mate(couple_two_all.at[beyond], couple_two_all.at[beyond], 19)
+
     inverse_load = pltpu.make_async_copy(inverse_hbm, inverse, local_sem.at[0])
     inverse_load.start()
     width = couple_two.shape[1]
@@ -242,11 +252,17 @@
     couple_two_all[r, :, width:] = transfer_two[...]
     trans_one_all[r] = transfer_one[...]
     top_rows[r, g] = couple_top[pl.ds(pl.multiple_of(g * slice_rows, slice_rows), slice_rows), :]
-    line_start(couple_two_all, 0, 0)
-
-    @pl.when(outer)
-    def _():
-        couple_end[0].start()
+
+    @pl.when(outer)
+    def _():
+        trans_end.start()
+        for c in couple_end[:2]:
+            c.start()
+
+    @pl.when(inner)
+    def _():
+        two_over.start()
+        two_own.start()
 
     tops = []
     for s in range(1, groups):
@@ -326,19 +342,19 @@
     @pl.when(outer)
     def _():
         proj_end.wait_send()
-        for c in couple_end[1:]:
+        for c in couple_end[2:]:
             c.start()
-        trans_end.start()
-
-    @pl.when(inner)
-    def _():
+        two_end.start()
+
+    @pl.when(inner)
+    def _():
+        two_over.wait_recv()
+        two_across.start()
         proj_from.wait_recv()
         proj_pass.start()
         proj_over.wait_recv()
         proj_pass.wait_recv()
 
-    line_wait(couple_two_all, 0, 0)
-    line_start(couple_two_all, 0, 1)
     for c in row_top:
         c.start()
 
@@ -346,13 +362,12 @@
     def _():
         stack_one = split(flat(proj_all[...]))
         solve_one[...] = dot3(split(couple_one[...]), stack_one)
+        reduced = matmul(transfer_one[...].T, solve_one[...])
         for c in couple_end:
             c.wait_recv()
+        trans_from.wait_recv()
         solve_ward[...] = dot3(split(couple_ward[...]), stack_one)
-        trans_from.wait_recv()
-        reduced = matmul(transfer_one[...].T, solve_one[...]) + matmul(
-            trans_one_all[mate].T, solve_ward[...]
-        )
+        reduced = reduced + matmul(trans_one_all[mate].T, solve_ward[...])
         for part in range(FAN):
             reduce_part[part] = reduced[:, part * part_cols : (part + 1) * part_cols]
         reduce_over.start()
@@ -369,16 +384,22 @@
     for c in quad_stack:
         c.start()
 
-    line_wait(couple_two_all, 0, 1)
-    line_start(couple_two_all, 0, 2)
-
-    @pl.when(inner)
-    def _():
-        solve_back.start()
+    @pl.when(inner)
+    def _():
+        two_from.wait_recv()
+        two_pass.start()
         trans_over.start()
         trans_pass.start()
-
-    line_wait(couple_two_all, 0, 2)
+        two_pass.wait_recv()
+        two_beyond.start()
+        solve_back.start()
+
+    @pl.when(outer)
+    def _():
+        two_own.wait_recv()
+        two_across.wait_recv()
+        two_beyond.wait_recv()
+
     trans_two_all[q] = couple_two_all[:, :, width:]
     quad_two = [
         over_quad(0, trans_two_all.at[q], trans_two_all.at[q], s) for s in range(1, FAN)
@@ -422,7 +443,7 @@
     for c in quad_block:
         c.wait_recv()
     fixed_two_all[r] = solve_two - dot3(gain_two, split(flat(block_two[...])))
-    line_start(fixed_two_all, 1, 0)
+    line_start(fixed_two_all, 0, 0)
 
     @pl.when(inner)
     def _():
@@ -433,11 +454,11 @@
         gain_back.start()
         gain_one[...] = dot3(split(couple_one[...]), trans_full)
 
-    line_wait(fixed_two_all, 1, 0)
-    line_start(fixed_two_all, 1, 1)
-    line_wait(fixed_two_all, 1, 1)
-    line_start(fixed_two_all, 1, 2)
-    line_wait(fixed_two_all, 1, 2)
+    line_wait(fixed_two_all, 0, 0)
+    line_start(fixed_two_all, 0, 1)
+    line_wait(fixed_two_all, 0, 1)
+    line_start(fixed_two_all, 0, 2)
+    line_wait(fixed_two_all, 0, 2)
 
     @pl.when(outer)
     def _():
@@ -449,7 +470,7 @@
         here = slice(part * part_cols, (part + 1) * part_cols)
         block_out[:, here] = solve_one[:, here] - dot3(gain, split(fixed_two_all[part]))
 
-    for which, buf in enumerate((couple_two_all, fixed_two_all)):
+    for which, buf in enumerate((fixed_two_all,)):
         line_finish(buf, which)
 
     @pl.when(outer)
@@ -457,12 +478,13 @@
         for c in couple_end:
             c.wait_send()
         trans_end.wait_send()
+        two_end.wait_send()
 
     @pl.when(inner)
     def _():
         for c in (
             proj_over, proj_pass, trans_over, trans_pass, reduce_over, reduce_ward,
-            solve_back, gain_back,
+            solve_back, gain_back, two_over, two_pass, two_own, two_across, two_beyond,
         ):
             c.wait_send()
 
@@ -470,10 +492,6 @@
         c.wait_send()
     placed_store.wait()
     spread_store.wait()
-
-
-def last(placed, spread, block, out):
-    out[...] = placed[...] - matmul(spread[...], block[...])
 
 
 def per_device(
@@ -503,7 +521,7 @@
         couple_two, transfer_two, couple_top,
     )
     placed, spread, block = pl.pallas_call(
-        functools.partial(kernel, depth, groups, leaf // 4),
+        functools.partial(kernel, depth, groups, leaf // TILES),
         out_shape=(
             jax.ShapeDtypeStruct((leaf, cols), F32),
             jax.ShapeDtypeStruct((leaf, rank), F32),
@@ -539,11 +557,11 @@
             pltpu.VMEM((rank, cols), F32),
             pltpu.VMEM((rank, rank), F32),
             pltpu.VMEM((rank, part_cols), F32),
-            dma((14,)),
-            dma((14,)),
+            dma((20,)),
+            dma((20,)),
             dma((3,)),
-            dma((2, 2, FAN - 1)),
-            dma((2, 2, FAN - 1)),
+            dma((1, 2, FAN - 1)),
+            dma((1, 2, FAN - 1)),
             dma((1, FAN - 1)),
             dma((1, FAN - 1)),
             dma((4, FAN - 1)),
@@ -557,19 +575,7 @@
             collective_id=0, has_side_effects=True, vmem_limit_bytes=56 * 1024 * 1024
         ),
     )(*args)
-    tile = leaf // 4
-    return pl.pallas_call(
-        last,
-        out_shape=jax.ShapeDtypeStruct((leaf, cols), F32),
-        grid=(leaf // tile,),
-        in_specs=[
-            pl.BlockSpec((tile, cols), lambda i: (i, 0)),
-            pl.BlockSpec((tile, rank), lambda i: (i, 0)),
-            pl.BlockSpec((rank, cols), lambda i: (0, 0)),
-        ],
-        out_specs=pl.BlockSpec((tile, cols), lambda i: (i, 0)),
-        compiler_params=pltpu.CompilerParams(vmem_limit_bytes=60 * 1024 * 1024),
-    )(placed, spread, block)
+    return placed - jnp.dot(spread, block, precision=lax.Precision.HIGH)
 
 
 def solution(mesh):

time: 116 us -> 117 us (level)
  matrix products: 0 us -> 4.4 us
  Pallas kernels: 116 us -> 113 us
    dot_general x0 -> x1, matrix products: none -> 4.4 us  [per_device(): return placed - jnp.dot(spread, block, precision=lax.Precision.HIGH)]
    pallas_call x2 -> x1, Pallas kernels: 116 us -> 113 us  [per_device(): pl.pallas_call(functools.partial(kernel, depth, groups, leaf // TILES), o...]
where the time goes in v3:
time: 117 us
  Pallas kernels  113 us (97%)
  matrix products  4.4 us (4%)
    pallas_call x1, Pallas kernels, per_device(): pl.pallas_call(functools.partial(kernel, depth, groups, leaf // TILES), o...  113 us
    dot_general x1, matrix products, per_device(): return placed - jnp.dot(spread, block, precision=lax.Precision.HIGH)  4.4 us

profile of v3, /device:TPU:0, one launch (start us, length us, event | category | flops | bytes accessed | tf_op | source)
XLA Modules:
  0.0 117.3 jit_solution(112732437170716843)
XLA Ops:
  0.0 112.9 %shard_map.91 = (f32[1024,512]{1,0:T(8,128)}, f32[1024,256]{1,0:T(8,128)}, f32[256,512]{1,0:T(8,128)}) custom-call(f32[1024,512]{1,0:T(8,128)} %labels.1, s32[1,1024]{1,0:T(1,128)} %order.1, f32[1024,1024]{1,0:T(8,128)} %inverse_hbm.1, f32[1024,256]{1,0:T(8,128)} %basis.1, f32[256,1024]{1,0:T(8,128)} %couple_one.1, f32[256,256]{1,0:T(8,128)} %transfer_one.1, ...), custom_call_target="tpu_custom_call" | custom-call | tf_op jit(solution)/shard_map/pallas_call | solution.py:523
  112.9 4.4 %convolution_subtract_fusion = f32[1024,512]{1,0:T(8,128)} fusion(f32[1024,512]{1,0:T(8,128)} %get-tuple-element.8, f32[1024,256]{1,0:T(8,128)} %get-tuple-element.9, f32[256,512]{1,0:T(8,128)} %get-tuple-element.10), kind=kOutput, calls=%fused_computation | convolution fusion | flops 805830656 | bytes 5767168 | tf_op jit(solution)/shard_map/dot_general | solution.py:578

commit v4 on v3

--- a/solution.py
+++ b/solution.py
@@ -10,7 +10,7 @@
 F32 = jnp.float32
 BF16 = jnp.bfloat16
 FAN = 4
-TILES = 1
+TILES = 2
 
 
 def split(x):
@@ -255,14 +255,15 @@
 
     @pl.when(outer)
     def _():
+        two_end.start()
         trans_end.start()
-        for c in couple_end[:2]:
-            c.start()
+        couple_end[0].start()
 
     @pl.when(inner)
     def _():
         two_over.start()
         two_own.start()
+        trans_over.start()
 
     tops = []
     for s in range(1, groups):
@@ -302,6 +303,11 @@
         value = dot3(split(inverse[rows, :]), (rhs_high[...], rhs_low[...]))
         sol_h[rows, :], sol_l[rows, :] = split(value)
 
+    @pl.when(inner)
+    def _():
+        two_from.wait_recv()
+        two_pass.start()
+
     proj_all[r] = dot3(split(basis[...].T), (sol_h[...], sol_l[...]))
 
     @pl.when(outer)
@@ -321,30 +327,11 @@
         value = dot3(split(inverse[rows, :]), (lab_high[:, :rank], lab_low[:, :rank]))
         rhs_high[rows, :rank], rhs_low[rows, :rank] = split(value)
 
-
-    @pl.loop(0, tiles)
-    def _(step):
-        rows = rows_of(step)
-        hot = (lax.broadcasted_iota(jnp.int32, (tile, leaf), 0) + step * tile) == order[...]
-        hot = hot.astype(F32).astype(BF16)
-        placed_out[rows, :] = dot(hot, sol_h[...]) + dot(hot, sol_l[...])
-        spread_out[rows, :] = dot(hot, rhs_high[:, :rank]) + dot(hot, rhs_low[:, :rank])
-
-    placed_store = pltpu.make_async_copy(placed_out, placed_hbm, local_sem.at[1])
-    spread_store = pltpu.make_async_copy(spread_out, spread_hbm, local_sem.at[2])
-    placed_store.start()
-    spread_store.start()
-
-    for c in tops:
-        c.wait_recv()
-    row_top = [over_row(0, top_rows.at[r], top_rows.at[r], s) for s in range(1, FAN)]
-
     @pl.when(outer)
     def _():
         proj_end.wait_send()
-        for c in couple_end[2:]:
+        for c in couple_end[1:]:
             c.start()
-        two_end.start()
 
     @pl.when(inner)
     def _():
@@ -352,10 +339,45 @@
         two_across.start()
         proj_from.wait_recv()
         proj_pass.start()
+
+    def hot_rows(step):
+        hot = (lax.broadcasted_iota(jnp.int32, (tile, leaf), 0) + step * tile) == order[...]
+        return hot.astype(F32).astype(BF16)
+
+    @pl.loop(0, tiles)
+    def _(step):
+        rows = rows_of(step)
+        hot = hot_rows(step)
+        placed_out[rows, :] = dot(hot, sol_h[...]) + dot(hot, sol_l[...])
+
+    placed_store = pltpu.make_async_copy(placed_out, placed_hbm, local_sem.at[1])
+    placed_store.start()
+
+    for c in tops:
+        c.wait_recv()
+    row_top = [over_row(0, top_rows.at[r], top_rows.at[r], s) for s in range(1, FAN)]
+
+    @pl.when(inner)
+    def _():
+        two_pass.wait_recv()
+        two_beyond.start()
         proj_over.wait_recv()
         proj_pass.wait_recv()
 
     for c in row_top:
+        c.start()
+
+    @pl.when(outer)
+    def _():
+        two_own.wait_recv()
+        two_across.wait_recv()
+        two_beyond.wait_recv()
+
+    trans_two_all[q] = couple_two_all[:, :, width:]
+    quad_two = [
+        over_quad(0, trans_two_all.at[q], trans_two_all.at[q], s) for s in range(1, FAN)
+    ]
+    for c in quad_two:
         c.start()
 
     @pl.when(inner)
@@ -386,30 +408,25 @@
 
     @pl.when(inner)
     def _():
-        two_from.wait_recv()
-        two_pass.start()
-        trans_over.start()
         trans_pass.start()
-        two_pass.wait_recv()
-        two_beyond.start()
         solve_back.start()
 
-    @pl.when(outer)
-    def _():
-        two_own.wait_recv()
-        two_across.wait_recv()
-        two_beyond.wait_recv()
-
-    trans_two_all[q] = couple_two_all[:, :, width:]
-    quad_two = [
-        over_quad(0, trans_two_all.at[q], trans_two_all.at[q], s) for s in range(1, FAN)
-    ]
-    for c in quad_two:
-        c.start()
+    @pl.loop(0, tiles)
+    def _(step):
+        rows = rows_of(step)
+        hot = hot_rows(step)
+        spread_out[rows, :] = dot(hot, rhs_high[:, :rank]) + dot(hot, rhs_low[:, :rank])
+
+    spread_store = pltpu.make_async_copy(spread_out, spread_hbm, local_sem.at[2])
+    spread_store.start()
+
     for c in row_top:
         c.wait_recv()
 
     couple = split(flat(couple_two_all[:, :, :width]))
+    for c in quad_two:
+        c.wait_recv()
+    gain_two = split(dot3(couple, split(flat(trans_two_all[...]))))
     own_two = flat(trans_two_all[q]).T
     for c in quad_stack:
         c.wait_recv()
@@ -420,9 +437,6 @@
     ]
     for c in quad_reduce:
         c.start()
-    for c in quad_two:
-        c.wait_recv()
-    gain_two = split(dot3(couple, split(flat(trans_two_all[...]))))
     for c in quad_reduce:
         c.wait_recv()
     top_all[sid] = top_part[q] + top_in[0] + (top_in[1] + top_in[2])

time: 117 us -> 109 us (0.932)
  Pallas kernels: 113 us -> 105 us
    pallas_call x1, Pallas kernels: 113 us -> 105 us  [per_device(): pl.pallas_call(functools.partial(kernel, depth, groups, leaf // TILES), o...]
where the time goes in v4:
time: 109 us
  Pallas kernels  105 us (96%)
  matrix products  4.4 us (4%)
    pallas_call x1, Pallas kernels, per_device(): pl.pallas_call(functools.partial(kernel, depth, groups, leaf // TILES), o...  105 us
    dot_general x1, matrix products, per_device(): return placed - jnp.dot(spread, block, precision=lax.Precision.HIGH)  4.4 us

profile of v4, /device:TPU:0, one launch (start us, length us, event | category | flops | bytes accessed | tf_op | source)
XLA Modules:
  0.0 109.1 jit_solution(13737006051745630416)
XLA Ops:
  0.0 104.7 %shard_map.91 = (f32[1024,512]{1,0:T(8,128)}, f32[1024,256]{1,0:T(8,128)}, f32[256,512]{1,0:T(8,128)}) custom-call(f32[1024,512]{1,0:T(8,128)} %labels.1, s32[1,1024]{1,0:T(1,128)} %order.1, f32[1024,1024]{1,0:T(8,128)} %inverse_hbm.1, f32[1024,256]{1,0:T(8,128)} %basis.1, f32[256,1024]{1,0:T(8,128)} %couple_one.1, f32[256,256]{1,0:T(8,128)} %transfer_one.1, ...), custom_call_target="tpu_custom_call" | custom-call | tf_op jit(solution)/shard_map/pallas_call | solution.py:537
  104.7 4.4 %convolution_subtract_fusion = f32[1024,512]{1,0:T(8,128)} fusion(f32[1024,512]{1,0:T(8,128)} %get-tuple-element.8, f32[1024,256]{1,0:T(8,128)} %get-tuple-element.9, f32[256,512]{1,0:T(8,128)} %get-tuple-element.10), kind=kOutput, calls=%fused_computation | convolution fusion | flops 805830656 | bytes 5767168 | tf_op jit(solution)/shard_map/dot_general | solution.py:592

commit v5 on v4

--- a/solution.py
+++ b/solution.py
@@ -48,10 +48,13 @@
     transfer_two,
     couple_top,
     placed_hbm,
-    spread_hbm,
-    block_out,
+    spread_high_hbm,
+    spread_low_hbm,
+    block_high,
+    block_low,
     placed_out,
-    spread_out,
+    spread_high,
+    spread_low,
     inverse,
     lab_high,
     lab_low,
@@ -69,7 +72,6 @@
     top_part,
     top_in,
     top_all,
-    block_two,
     top_rows,
     solve_one,
     gain_one,
@@ -251,7 +253,7 @@
     couple_two_all[r, :, :width] = couple_two[...]
     couple_two_all[r, :, width:] = transfer_two[...]
     trans_one_all[r] = transfer_one[...]
-    top_rows[r, g] = couple_top[pl.ds(pl.multiple_of(g * slice_rows, slice_rows), slice_rows), :]
+    top_rows[q, r, g] = couple_top[pl.ds(pl.multiple_of(g * slice_rows, slice_rows), slice_rows), :]
 
     @pl.when(outer)
     def _():
@@ -271,7 +273,7 @@
         tops.append(
             over_tops(
                 couple_top.at[pl.ds(pl.multiple_of(other * slice_rows, slice_rows), slice_rows)],
-                top_rows.at[r, g],
+                top_rows.at[q, r, g],
                 s,
             )
         )
@@ -355,7 +357,9 @@
 
     for c in tops:
         c.wait_recv()
-    row_top = [over_row(0, top_rows.at[r], top_rows.at[r], s) for s in range(1, FAN)]
+    row_top = [over_row(0, top_rows.at[q, r], top_rows.at[q, r], s) for s in range(1, FAN)]
+    for c in row_top:
+        c.start()
 
     @pl.when(inner)
     def _():
@@ -363,9 +367,6 @@
         two_beyond.start()
         proj_over.wait_recv()
         proj_pass.wait_recv()
-
-    for c in row_top:
-        c.start()
 
     @pl.when(outer)
     def _():
@@ -378,6 +379,12 @@
         over_quad(0, trans_two_all.at[q], trans_two_all.at[q], s) for s in range(1, FAN)
     ]
     for c in quad_two:
+        c.start()
+
+    for c in row_top:
+        c.wait_recv()
+    quad_top = [over_quad(3, top_rows.at[q], top_rows.at[q], s) for s in range(1, FAN)]
+    for c in quad_top:
         c.start()
 
     @pl.when(inner)
@@ -415,13 +422,16 @@
     def _(step):
         rows = rows_of(step)
         hot = hot_rows(step)
-        spread_out[rows, :] = dot(hot, rhs_high[:, :rank]) + dot(hot, rhs_low[:, :rank])
-
-    spread_store = pltpu.make_async_copy(spread_out, spread_hbm, local_sem.at[2])
-    spread_store.start()
-
-    for c in row_top:
-        c.wait_recv()
+        spread_high[rows, :] = dot(hot, rhs_high[:, :rank]).astype(BF16)
+        spread_low[rows, :] = dot(hot, rhs_low[:, :rank]).astype(BF16)
+
+    spread_store = [
+        pltpu.make_async_copy(spread_high, spread_high_hbm, local_sem.at[2]),
+        pltpu.make_async_copy(spread_low, spread_low_hbm, local_sem.at[3]),
+    ]
+    for c in spread_store:
+        c.start()
+
 
     couple = split(flat(couple_two_all[:, :, :width]))
     for c in quad_two:
@@ -445,18 +455,14 @@
         c.start()
     for c in wide_top:
         c.wait_recv()
-    total = jnp.zeros((part_rows, part_cols), F32)
+    for c in quad_top:
+        c.wait_recv()
+    total = jnp.zeros((rank, part_cols), F32)
     for other in range(groups):
         total = total + matmul(
-            flat(top_rows[:, other]), flat(top_all[other * FAN : (other + 1) * FAN])
-        )
-    block_two[q] = total
-    quad_block = [over_quad(3, block_two.at[q], block_two.at[q], s) for s in range(1, FAN)]
-    for c in quad_block:
-        c.start()
-    for c in quad_block:
-        c.wait_recv()
-    fixed_two_all[r] = solve_two - dot3(gain_two, split(flat(block_two[...])))
+            flat(top_rows[:, :, other]), flat(top_all[other * FAN : (other + 1) * FAN])
+        )
+    fixed_two_all[r] = solve_two - dot3(gain_two, split(total))
     line_start(fixed_two_all, 0, 0)
 
     @pl.when(inner)
@@ -482,7 +488,8 @@
     gain = split(gain_one[...])
     for part in range(FAN):
         here = slice(part * part_cols, (part + 1) * part_cols)
-        block_out[:, here] = solve_one[:, here] - dot3(gain, split(fixed_two_all[part]))
+        value = solve_one[:, here] - dot3(gain, split(fixed_two_all[part]))
+        block_high[:, here], block_low[:, here] = split(value)
 
     for which, buf in enumerate((fixed_two_all,)):
         line_finish(buf, which)
@@ -502,10 +509,17 @@
         ):
             c.wait_send()
 
-    for c in tops + row_top + quad_two + quad_stack + quad_reduce + wide_top + quad_block:
+    for c in tops + row_top + quad_two + quad_stack + quad_reduce + wide_top + quad_top:
         c.wait_send()
     placed_store.wait()
-    spread_store.wait()
+    for c in spread_store:
+        c.wait()
+
+
+def last(placed, spread_high, spread_low, block_high, block_low, out):
+    out[...] = placed[...] - dot3(
+        (spread_high[...], spread_low[...]), (block_high[...], block_low[...])
+    )
 
 
 def per_device(
@@ -534,18 +548,21 @@
         labels, point_order, leaf_inverse, leaf_basis, couple_one, transfer_one,
         couple_two, transfer_two, couple_top,
     )
-    placed, spread, block = pl.pallas_call(
+    placed, *parts = pl.pallas_call(
         functools.partial(kernel, depth, groups, leaf // TILES),
         out_shape=(
             jax.ShapeDtypeStruct((leaf, cols), F32),
-            jax.ShapeDtypeStruct((leaf, rank), F32),
-            jax.ShapeDtypeStruct((rank, cols), F32),
+            jax.ShapeDtypeStruct((leaf, rank), BF16),
+            jax.ShapeDtypeStruct((leaf, rank), BF16),
+            jax.ShapeDtypeStruct((rank, cols), BF16),
+            jax.ShapeDtypeStruct((rank, cols), BF16),
         ),
         in_specs=[vmem, vmem, far] + [vmem] * (len(args) - 3),
-        out_specs=(far, far, vmem),
+        out_specs=(far, far, far, vmem, vmem),
         scratch_shapes=[
             pltpu.VMEM((leaf, cols), F32),
-            pltpu.VMEM((leaf, rank), F32),
+            pltpu.VMEM((leaf, rank), BF16),
+            pltpu.VMEM((leaf, rank), BF16),
             pltpu.VMEM((leaf, leaf), F32),
             pltpu.VMEM((leaf, cols), BF16),
             pltpu.VMEM((leaf, cols), BF16),
@@ -563,8 +580,7 @@
             pltpu.VMEM((FAN, part_rows, part_cols), F32),
             pltpu.VMEM((FAN - 1, part_rows, part_cols), F32),
             pltpu.VMEM((wide, part_rows, part_cols), F32),
-            pltpu.VMEM((FAN, part_rows, part_cols), F32),
-            pltpu.VMEM((FAN, groups, slice_rows, rank), F32),
+            pltpu.VMEM((FAN, FAN, groups, slice_rows, rank), F32),
             pltpu.VMEM((rank, cols), F32),
             pltpu.VMEM((rank, rank), F32),
             pltpu.VMEM(couple_one.shape, F32),
@@ -573,7 +589,7 @@
             pltpu.VMEM((rank, part_cols), F32),
             dma((20,)),
             dma((20,)),
-            dma((3,)),
+            dma((4,)),
             dma((1, 2, FAN - 1)),
             dma((1, 2, FAN - 1)),
             dma((1, FAN - 1)),
@@ -589,7 +605,20 @@
             collective_id=0, has_side_effects=True, vmem_limit_bytes=56 * 1024 * 1024
         ),
     )(*args)
-    return placed - jnp.dot(spread, block, precision=lax.Precision.HIGH)
+    tile = leaf // 4
+    spread_spec = pl.BlockSpec((tile, rank), lambda i: (i, 0))
+    block_spec = pl.BlockSpec((rank, cols), lambda i: (0, 0))
+    return pl.pallas_call(
+        last,
+        out_shape=jax.ShapeDtypeStruct((leaf, cols), F32),
+        grid=(leaf // tile,),
+        in_specs=[
+            pl.BlockSpec((tile, cols), lambda i: (i, 0)),
+            spread_spec, spread_spec, block_spec, block_spec,
+        ],
+        out_specs=pl.BlockSpec((tile, cols), lambda i: (i, 0)),
+        compiler_params=pltpu.CompilerParams(vmem_limit_bytes=60 * 1024 * 1024),
+    )(placed, *parts)
 
 
 def solution(mesh):

time: 109 us -> 107 us (0.982)
  matrix products: 4.4 us -> 0 us
  Pallas kernels: 105 us -> 107 us
    pallas_call x0 -> x1, Pallas kernels: none -> 4.85 us  [per_device(): pl.pallas_call(last, out_shape=jax.ShapeDtypeStruct((leaf, cols), F32), g...]
    dot_general x1 -> x0, matrix products: 4.4 us -> none  [per_device(): return placed - jnp.dot(spread, block, precision=lax.Precision.HIGH)]
    pallas_call x1, Pallas kernels: 105 us -> 102 us  [per_device(): pl.pallas_call(functools.partial(kernel, depth, groups, leaf // TILES), o...]
where the time goes in v5:
time: 107 us
  Pallas kernels  107 us (100%)
    pallas_call x1, Pallas kernels, per_device(): pl.pallas_call(functools.partial(kernel, depth, groups, leaf // TILES), o...  102 us
    pallas_call x1, Pallas kernels, per_device(): pl.pallas_call(last, out_shape=jax.ShapeDtypeStruct((leaf, cols), F32), g...  4.85 us

profile of v5, /device:TPU:0, one launch (start us, length us, event | category | flops | bytes accessed | tf_op | source)
XLA Modules:
  0.0 107.1 jit_solution(5097631224302469185)
XLA Ops:
  0.0 102.2 %shard_map.91 = (f32[1024,512]{1,0:T(8,128)}, bf16[1024,256]{1,0:T(8,128)(2,1)}, bf16[1024,256]{1,0:T(8,128)(2,1)}, bf16[256,512]{1,0:T(8,128)(2,1)}, bf16[256,512]{1,0:T(8,128)(2,1)}) custom-call(f32[1024,512]{1,0:T(8,128)} %labels.1, s32[1,1024]{1,0:T(1,128)} %order.1, f32[1024,1024]{1,0:T(8,128)} %inverse_hbm.1, f32[1024,256]{1,0:T(8,128)} %basis.1, ...), custom_call_target="tpu_custom_call" | custom-call | tf_op jit(solution)/shard_map/pallas_call | solution.py:551
  102.3 4.8 %shard_map.92 = f32[1024,512]{1,0:T(8,128)} custom-call(f32[1024,512]{1,0:T(8,128)} %get-tuple-element.10.placed, bf16[1024,256]{1,0:T(8,128)(2,1)} %get-tuple-element.11.spread_high, bf16[1024,256]{1,0:T(8,128)(2,1)} %get-tuple-element.12.spread_low, bf16[256,512]{1,0:T(8,128)(2,1)} %get-tuple-element.13.block_high, ...), custom_call_target="tpu_custom_call" | custom-call | tf_op jit(solution)/shard_map/pallas_call | solution.py:611

commit v6 on v5

--- a/solution.py
+++ b/solution.py
@@ -389,17 +389,30 @@
 
     @pl.when(inner)
     def _():
-        stack_one = split(flat(proj_all[...]))
-        solve_one[...] = dot3(split(couple_one[...]), stack_one)
-        reduced = matmul(transfer_one[...].T, solve_one[...])
+        own_couple = split(couple_one[...])
+        own_trans = split(transfer_one[...].T)
         for c in couple_end:
             c.wait_recv()
         trans_from.wait_recv()
-        solve_ward[...] = dot3(split(couple_ward[...]), stack_one)
-        reduced = reduced + matmul(trans_one_all[mate].T, solve_ward[...])
-        for part in range(FAN):
-            reduce_part[part] = reduced[:, part * part_cols : (part + 1) * part_cols]
+        ward_couple = split(couple_ward[...])
+        ward_trans = split(trans_one_all[mate].T)
+
+        def level_one(pair):
+            here = pl.ds(pl.multiple_of(pair * 2 * part_cols, 2 * part_cols), 2 * part_cols)
+            stack_one = split(flat(proj_all[:, :, here]))
+            own = dot3(own_couple, stack_one)
+            ward = dot3(ward_couple, stack_one)
+            solve_one[:, here] = own
+            solve_ward[:, here] = ward
+            reduced = dot3(own_trans, split(own)) + dot3(ward_trans, split(ward))
+            for part in range(2):
+                reduce_part[pair * 2 + part] = reduced[
+                    :, part * part_cols : (part + 1) * part_cols
+                ]
+
+        level_one(1 - r // 2)
         reduce_over.start()
+        level_one(r // 2)
         reduce_over.wait_recv()
         ward_part[...] = reduce_part[mate] + reduce_in[mate % 2]
         reduce_ward.start()
@@ -409,9 +422,20 @@
     def _():
         reduce_ward.wait_recv()
 
-    quad_stack = [over_quad(1, stack_two.at[q], stack_two.at[q], s) for s in range(1, FAN)]
-    for c in quad_stack:
-        c.start()
+    beside = q + 1 - 2 * (q % 2)
+    opposite = (q + 2) % FAN
+
+    def stack_copy(slot, to, number):
+        return copy(
+            stack_two.at[slot], stack_two.at[slot], quad_send.at[1, number],
+            quad_recv.at[1, number], device(g * FAN + to, r),
+        )
+
+    quad_stack = [
+        stack_copy(q, opposite, 0), stack_copy(q, beside, 1), stack_copy(opposite, beside, 2)
+    ]
+    quad_stack[0].start()
+    quad_stack[1].start()
 
     @pl.when(inner)
     def _():
@@ -433,12 +457,14 @@
         c.start()
 
 
+    quad_stack[0].wait_recv()
+    quad_stack[2].start()
     couple = split(flat(couple_two_all[:, :, :width]))
     for c in quad_two:
         c.wait_recv()
     gain_two = split(dot3(couple, split(flat(trans_two_all[...]))))
     own_two = flat(trans_two_all[q]).T
-    for c in quad_stack:
+    for c in quad_stack[1:]:
         c.wait_recv()
     solve_two = dot3(couple, split(flat(stack_two[...])))
     top_part[...] = matmul(own_two, solve_two).reshape(FAN, part_rows, part_cols)

time: 107 us -> 107 us (level)
  no operation moved by 1% of the time
where the time goes in v6:
time: 107 us
  Pallas kernels  107 us (100%)
    pallas_call x1, Pallas kernels, per_device(): pl.pallas_call(functools.partial(kernel, depth, groups, leaf // TILES), o...  102 us
    pallas_call x1, Pallas kernels, per_device(): pl.pallas_call(last, out_shape=jax.ShapeDtypeStruct((leaf, cols), F32), g...  4.85 us

profile of v6, /device:TPU:0, one launch (start us, length us, event | category | flops | bytes accessed | tf_op | source)
XLA Modules:
  0.0 106.8 jit_solution(16713221792813563185)
XLA Ops:
  0.0 102.0 %shard_map.91 = (f32[1024,512]{1,0:T(8,128)}, bf16[1024,256]{1,0:T(8,128)(2,1)}, bf16[1024,256]{1,0:T(8,128)(2,1)}, bf16[256,512]{1,0:T(8,128)(2,1)}, bf16[256,512]{1,0:T(8,128)(2,1)}) custom-call(f32[1024,512]{1,0:T(8,128)} %labels.1, s32[1,1024]{1,0:T(1,128)} %order.1, f32[1024,1024]{1,0:T(8,128)} %inverse_hbm.1, f32[1024,256]{1,0:T(8,128)} %basis.1, ...), custom_call_target="tpu_custom_call" | custom-call | tf_op jit(solution)/shard_map/pallas_call | solution.py:577
  102.0 4.8 %shard_map.92 = f32[1024,512]{1,0:T(8,128)} custom-call(f32[1024,512]{1,0:T(8,128)} %get-tuple-element.10.placed, bf16[1024,256]{1,0:T(8,128)(2,1)} %get-tuple-element.11.spread_high, bf16[1024,256]{1,0:T(8,128)(2,1)} %get-tuple-element.12.spread_low, bf16[256,512]{1,0:T(8,128)(2,1)} %get-tuple-element.13.block_high, ...), custom_call_target="tpu_custom_call" | custom-call | tf_op jit(solution)/shard_map/pallas_call | solution.py:637
